TPU v7x, 32 devices: a whole 2x2x4 slice. The times are simulated.
32 devices in a mesh: pipe: 2 (over y), dp: 4 (over z), tensor: 4 (over x, core).
Axes of the slice: x: 2, y: 2, z: 4, core: 2. Of those that a mesh axis runs over, the one named last changes fastest.
Arguments:
- acts_in: bfloat16 [8, 1024, 1024], P('dp', 'tensor'), may hold values from -6 to 6
- out_grad: bfloat16 [8, 1024, 1024], P('dp', 'tensor'), may hold values from -6 to 6
- mix_gain: bfloat16 [2, 1024], P('pipe', 'dp'), may hold values from 0.5 to 1.5
- w_mixer_in: bfloat16 [2, 1024, 2, 1536], P('pipe', 'dp', None, 'tensor'), may hold values from -0.1875 to 0.1875
- w_query: bfloat16 [2, 1024, 512], P('pipe', 'dp', 'tensor'), may hold values from -0.1875 to 0.1875
- w_shared: bfloat16 [2, 1024, 512], P('pipe', 'dp'), may hold values from -0.1875 to 0.1875
- w_step: bfloat16 [2, 1024, 24], P('pipe', 'dp'), may hold values from -0.1875 to 0.1875
- a_log: float32 [2, 24], P('pipe', 'tensor'), may hold values from 0 to 2.77
- dt_bias: float32 [2, 24], P('pipe', 'tensor'), may hold values from -7 to -2.3
- d_skip: float32 [2, 24], P('pipe', 'tensor'), may hold values from 0.5 to 1.5
- w_mamba_out: bfloat16 [2, 1536, 1024], P('pipe', 'tensor', 'dp'), may hold values from -0.3125 to 0.3125
- w_attn_out: bfloat16 [2, 512, 1024], P('pipe', 'tensor', 'dp'), may hold values from -1.5 to 1.5
- ffn_gain: bfloat16 [2, 1024], P('pipe', 'dp'), may hold values from 0.5 to 1.5
- w_gate_up: bfloat16 [2, 1024, 2, 2048], P('pipe', 'dp', None, 'tensor'), may hold values from -0.1875 to 0.1875
- w_down: bfloat16 [2, 2048, 1024], P('pipe', 'tensor', 'dp'), may hold values from -0.25 to 0.25
Outputs:
- acts_out: bfloat16 [2, 8, 1024, 1024], P('pipe', 'dp', 'tensor')
- in_grads: bfloat16 [2, 8, 1024, 1024], P('pipe', 'dp', 'tensor')
- grad_gains: float32 [2, 2, 1024], P('pipe', None, ('dp', 'tensor'))
- grad_mixer_in: float32 [2, 1024, 2, 1536], P('pipe', 'dp', None, 'tensor')
- grad_query: float32 [2, 1024, 512], P('pipe', 'dp', 'tensor')
- grad_shared: float32 [2, 1024, 512], P('pipe', ('dp', 'tensor'))
- grad_step: float32 [2, 1024, 24], P('pipe', ('dp', 'tensor'))
- grad_heads: float32 [2, 3, 24], P('pipe', None, 'tensor')
- grad_mamba_out: float32 [2, 1536, 1024], P('pipe', 'tensor', 'dp')
- grad_attn_out: float32 [2, 512, 1024], P('pipe', 'tensor', 'dp')
- grad_gate_up: float32 [2, 1024, 2, 2048], P('pipe', 'dp', None, 'tensor')
- grad_down: float32 [2, 2048, 1024], P('pipe', 'tensor', 'dp')
All inputs are finite; a program needn't handle non-finite values.
Results may differ from a plain program's by a relative error of at most 0.04.
Values may be sent and summed in bfloat16 or wider, within the bound.
A program may use at most 256 MiB of HBM per device.

v0:
```python
import functools

import jax
import jax.numpy as jnp
from jax import lax
from jax.experimental import pallas as pl
from jax.experimental.pallas import tpu as pltpu
from jax.sharding import PartitionSpec as P

HM = 24
HA = 8
KVH = 2
NS = 128
HD = 64
LANES = 128
STEP = 128
TILE = 256
EPS = 1e-05
F32 = jnp.float32
B16 = jnp.bfloat16
VMEM_LIMIT = 60 << 20


def nn(a, b):
    return lax.dot_general(a, b, (((1,), (0,)), ((), ())), preferred_element_type=F32)


def nt(a, b):
    return lax.dot_general(a, b, (((1,), (1,)), ((), ())), preferred_element_type=F32)


def tn(a, b):
    return lax.dot_general(a, b, (((0,), (0,)), ((), ())), preferred_element_type=F32)


def exact(a, b):
    return lax.dot_general(
        a, b, (((1,), (0,)), ((), ())), precision=lax.Precision.HIGHEST, preferred_element_type=F32
    )


def softplus(v):
    small = jnp.exp(-jnp.abs(v))
    series = small * (1.0 - small * (0.5 - small * (1.0 / 3.0 - small * 0.25)))
    return jnp.maximum(v, 0.0) + jnp.where(small < 0.02, series, jnp.log(1.0 + small))


def sigmoid(v):
    return 1.0 / (1.0 + jnp.exp(-v))


def iotas(rows, columns):
    return (
        lax.broadcasted_iota(jnp.int32, (rows, columns), 0),
        lax.broadcasted_iota(jnp.int32, (rows, columns), 1),
    )


def spread(column_block, head, rows):
    return jnp.broadcast_to(column_block[:, head : head + 1], (rows, LANES))


class Cols:
    def __init__(self, width):
        self.width = width
        self.z = 0
        self.u = width
        self.q = 2 * width
        self.b = self.q + LANES
        self.c = self.b + LANES
        self.k = self.c + LANES
        self.v = self.k + LANES
        self.step = self.v + LANES
        self.total = self.step + LANES
        self.pairs = width // LANES


def split_heads(block, low_lanes):
    zero = jnp.zeros_like(block)
    return jnp.concatenate(
        [jnp.where(low_lanes, block, zero), jnp.where(low_lanes, zero, block)], axis=0
    )


def core_fwd_kernel(
    cols, rows_ref, wcat_ref, wout_ref, hp_ref, dsk_ref,
    proj_ref, step_ref, y_ref, lows_ref, states_ref, lse_ref, part_ref, state,
):
    length = rows_ref.shape[0]
    width = cols.width

    def project(i, _):
        rows = pl.ds(pl.multiple_of(i * TILE, TILE), TILE)
        block = rows_ref[rows, :]
        for first in range(0, cols.total, 512):
            last = min(first + 512, cols.total)
            value = nn(block, wcat_ref[:, first:last])
            if last == cols.total:
                step_ref[rows, :] = value[:, cols.step - first :]
                value = value[:, : cols.step - first]
                last = cols.step
            if first <= cols.q < last:
                at = cols.q - first
                value = jnp.concatenate(
                    [value[:, :at], value[:, at : at + LANES] * HD**-0.5, value[:, at + LANES :]],
                    axis=1,
                ) if at else jnp.concatenate(
                    [value[:, :LANES] * HD**-0.5, value[:, LANES:]], axis=1
                )
            proj_ref[rows, first:last] = value.astype(B16)
        return 0

    lax.fori_loop(0, length // TILE, project, 0)

    ri, ci = iotas(STEP, STEP)
    lower = ri >= ci
    tril = lower.astype(F32)
    low_lanes = ci < HD
    decay = jnp.exp(hp_ref[0:1, :])
    bias = hp_ref[1:2, :]
    state[...] = jnp.zeros_like(state)

    def scan_block(b, _):
        rows = pl.ds(pl.multiple_of(b * STEP, STEP), STEP)
        dt = softplus(step_ref[rows, :] + bias)
        run = exact(tril, -dt * decay)
        run_t = run.T
        bm = proj_ref[rows, cols.b : cols.b + LANES]
        cm = proj_ref[rows, cols.c : cols.c + LANES]
        cb = jnp.where(lower, nt(cm, bm), 0.0)
        states_in = state[...]
        low_state = states_in.astype(B16)
        states_ref[b] = low_state
        carried = nn(cm, low_state)
        tails, fades = [], []
        for p in range(cols.pairs):
            lanes = slice(LANES * p, LANES * (p + 1))
            u = proj_ref[rows, cols.u + LANES * p : cols.u + LANES * (p + 1)].astype(F32)
            z = proj_ref[rows, cols.z + LANES * p : cols.z + LANES * (p + 1)].astype(F32)
            run_b = [spread(run, 2 * p + k, STEP) for k in range(2)]
            run_w = jnp.where(low_lanes, run_b[0], run_b[1])
            ud = u * jnp.where(low_lanes, spread(dt, 2 * p, STEP), spread(dt, 2 * p + 1, STEP))
            mix = jnp.concatenate(
                [
                    (
                        jnp.exp(jnp.minimum(run_b[k] - run_t[2 * p + k : 2 * p + k + 1, :], 0.0))
                        * cb
                    ).astype(B16)
                    for k in range(2)
                ],
                axis=1,
            )
            inside = nn(mix, split_heads(ud, low_lanes).astype(B16))
            y = inside + carried[:, lanes] * jnp.exp(run_w) + dsk_ref[0:1, lanes] * u
            y_ref[rows, lanes] = y.astype(B16)
            lows_ref[rows, lanes] = (y * z * sigmoid(z)).astype(B16)
            end = run_w[STEP - 1 : STEP, :]
            tails.append((ud * jnp.exp(end - run_w)).astype(B16))
            fades.append(jnp.exp(end))
        fresh = tn(bm, jnp.concatenate(tails, axis=1))
        state[...] = states_in * jnp.concatenate(fades, axis=1) + fresh
        return 0

    lax.fori_loop(0, length // STEP, scan_block, 0)

    rk, ck = iotas(TILE, 2 * TILE)
    diagonal = rk <= jnp.where(ck < TILE, ck, ck - TILE)
    q_low = iotas(TILE, LANES)[1] < HD

    def attend(i, _):
        rows = pl.ds(pl.multiple_of(i * TILE, TILE), TILE)
        q2 = split_heads(proj_ref[rows, cols.q : cols.q + LANES], q_low)

        def piece(j, carry, masked):
            top, total, out = carry
            keys = pl.ds(pl.multiple_of(j * TILE, TILE), TILE)
            s = nt(proj_ref[keys, cols.k : cols.k + LANES], q2)
            if masked:
                s = jnp.where(diagonal, s, -1e30)
            new_top = jnp.maximum(top, jnp.max(s, axis=0, keepdims=True))
            p = jnp.exp(s - new_top)
            scale = jnp.exp(top - new_top)
            total = total * scale + jnp.sum(p, axis=0, keepdims=True)
            out = out * scale + tn(proj_ref[keys, cols.v : cols.v + LANES], p.astype(B16))
            return new_top, total, out

        carry = (
            jnp.full((1, 2 * TILE), -1e30, F32),
            jnp.zeros((1, 2 * TILE), F32),
            jnp.zeros((LANES, 2 * TILE), F32),
        )
        carry = lax.fori_loop(0, i, lambda j, c: piece(j, c, False), carry)
        top, total, out = piece(i, carry, True)
        out = out / total
        joined = jnp.concatenate([out[:HD, :TILE], out[HD:, TILE:]], axis=0)
        lows_ref[rows, width : width + LANES] = joined.T.astype(B16)
        lse_ref[i] = jnp.broadcast_to(top + jnp.log(total), (8, 2 * TILE))
        return 0

    lax.fori_loop(0, length // TILE, attend, 0)
    multiply_out(lows_ref, wout_ref, part_ref)


def multiply_out(lows_ref, wout_ref, part_ref):
    ways, _, piece = wout_ref.shape

    def out_rows(i, _):
        rows = pl.ds(pl.multiple_of(i * TILE, TILE), TILE)
        block = lows_ref[rows, :]
        for k in range(ways):
            part_ref[rows, k * piece : (k + 1) * piece] = nn(block, wout_ref[k]).astype(B16)
        return 0

    lax.fori_loop(0, lows_ref.shape[0] // TILE, out_rows, 0)


def core_bwd_kernel(
    cols, back_ref, wcat_ref, wout_ref, hp_ref, dsk_ref, group_ref, proj_ref, step_ref, y_ref, lows_ref,
    states_ref, lse_ref,
    dproj_ref, heads_ref, part_ref, dcore, grad_state, skip_sum, dk_sum, dv_sum,
):
    length = back_ref.shape[0]
    width = cols.width
    ways, _, piece = wout_ref.shape
    blocks = length // STEP

    def into_core(i, _):
        rows = pl.ds(pl.multiple_of(i * TILE, TILE), TILE)
        total = nt(back_ref[rows, 0:piece], wout_ref[0])
        for k in range(1, ways):
            total += nt(back_ref[rows, k * piece : (k + 1) * piece], wout_ref[k])
        dcore[rows, :] = total.astype(B16)
        return 0

    lax.fori_loop(0, length // TILE, into_core, 0)

    rk, ck = iotas(TILE, 2 * TILE)
    diagonal = rk <= jnp.where(ck < TILE, ck, ck - TILE)
    q_low = iotas(TILE, LANES)[1] < HD
    dk_sum[...] = jnp.zeros_like(dk_sum)
    dv_sum[...] = jnp.zeros_like(dv_sum)
    half = iotas(8, LANES)
    pick_low = (half[1] < HD).astype(F32)
    pick_high = (half[1] >= HD).astype(F32)

    def attend(i, _):
        rows = pl.ds(pl.multiple_of(i * TILE, TILE), TILE)
        q2 = split_heads(proj_ref[rows, cols.q : cols.q + LANES], q_low)
        d_out = dcore[rows, width : width + LANES]
        do2 = split_heads(d_out, q_low)
        both = d_out.astype(F32) * lows_ref[rows, width : width + LANES].astype(F32)
        high = lax.Precision.HIGHEST
        deltas = [
            lax.dot_general(
                pick, both, (((1,), (1,)), ((), ())), precision=high, preferred_element_type=F32
            )[0:1, :]
            for pick in (pick_low, pick_high)
        ]
        delta = jnp.concatenate(deltas, axis=1)
        lse = lse_ref[i][0:1, :]

        def piece_of(j, dq, masked):
            keys = pl.ds(pl.multiple_of(j * TILE, TILE), TILE)
            kk = proj_ref[keys, cols.k : cols.k + LANES]
            p = jnp.exp(nt(kk, q2) - lse)
            if masked:
                p = jnp.where(diagonal, p, 0.0)
            ds = (p * (nt(proj_ref[keys, cols.v : cols.v + LANES], do2) - delta)).astype(B16)
            dv_sum[keys, :] += nn(p.astype(B16), do2)
            dk_sum[keys, :] += nn(ds, q2)
            return dq + tn(kk, ds)

        dq = jnp.zeros((LANES, 2 * TILE), F32)
        dq = lax.fori_loop(0, i, lambda j, c: piece_of(j, c, False), dq)
        dq = piece_of(i, dq, True)
        joined = jnp.concatenate([dq[:HD, :TILE], dq[HD:, TILE:]], axis=0) * HD**-0.5
        dproj_ref[rows, cols.q : cols.q + LANES] = joined.T.astype(B16)
        return 0

    lax.fori_loop(0, length // TILE, attend, 0)
    dproj_ref[:, cols.k : cols.k + LANES] = dk_sum[...].astype(B16)
    dproj_ref[:, cols.v : cols.v + LANES] = dv_sum[...].astype(B16)

    ri, ci = iotas(STEP, STEP)
    upper = ri <= ci
    tril = (ri >= ci).astype(F32)
    triu = upper.astype(F32)
    low_lanes = ci < HD
    decay = jnp.exp(hp_ref[0:1, :])
    bias = hp_ref[1:2, :]
    grad_state[...] = jnp.zeros_like(grad_state)
    skip_sum[...] = jnp.zeros_like(skip_sum)
    heads_ref[...] = jnp.zeros_like(heads_ref)
    zero_rows = jnp.zeros((STEP - 2 * cols.pairs, LANES), F32)

    def scan_block(back, _):
        b = blocks - 1 - back
        rows = pl.ds(pl.multiple_of(b * STEP, STEP), STEP)
        raw = step_ref[rows, :] + bias
        dt = softplus(raw)
        a = -dt * decay
        run = exact(tril, a)
        run_t = run.T
        bm = proj_ref[rows, cols.b : cols.b + LANES]
        cm = proj_ref[rows, cols.c : cols.c + LANES]
        cbt = jnp.where(upper, nt(bm, cm), 0.0)
        low_state = states_ref[b]
        grads_out = grad_state[...]
        low_grad = grads_out.astype(B16)
        carried = nn(cm, low_state)
        pulled = nn(bm, low_grad)
        dcb = jnp.zeros((STEP, STEP), F32)
        dy_fades, u_tails, fades = [], [], []
        carry_terms, direct_terms, tail_terms = [], [], []
        row_sums = []
        col_sums = jnp.zeros((STEP, LANES), F32)
        for p in range(cols.pairs):
            lanes = slice(LANES * p, LANES * (p + 1))
            u16 = proj_ref[rows, cols.u + LANES * p : cols.u + LANES * (p + 1)]
            u = u16.astype(F32)
            z = proj_ref[rows, cols.z + LANES * p : cols.z + LANES * (p + 1)].astype(F32)
            y = y_ref[rows, lanes].astype(F32)
            dm = dcore[rows, lanes].astype(F32)
            sg = sigmoid(z)
            dy = dm * z * sg
            dproj_ref[rows, cols.z + LANES * p : cols.z + LANES * (p + 1)] = (
                dm * y * sg * (1.0 + z * (1.0 - sg))
            ).astype(B16)
            dy16 = dy.astype(B16)
            skip_sum[:, lanes] += u * dy
            run_b = [spread(run, 2 * p + k, STEP) for k in range(2)]
            dt_b = [spread(dt, 2 * p + k, STEP) for k in range(2)]
            run_w = jnp.where(low_lanes, run_b[0], run_b[1])
            dt_w = jnp.where(low_lanes, dt_b[0], dt_b[1])
            end = run_w[STEP - 1 : STEP, :]
            fade = jnp.exp(run_w)
            tail = jnp.exp(end - run_w)
            dmix = nt(split_heads(u16, low_lanes), dy16)
            mixes = []
            for k in range(2):
                gap = jnp.exp(jnp.minimum(run_t[2 * p + k : 2 * p + k + 1, :] - run_b[k], 0.0))
                mixes.append((gap * cbt).astype(B16))
                weighted = gap * dt_b[k] * dmix[STEP * k : STEP * (k + 1), :]
                dcb += weighted
                moved = weighted * cbt
                row_sums.append(jnp.sum(moved, axis=0, keepdims=True))
                col_sums = jnp.where(
                    ci == 2 * p + k, jnp.sum(moved, axis=1, keepdims=True), col_sums
                )
            inside = nn(jnp.concatenate(mixes, axis=1), split_heads(dy16, low_lanes))
            pull_tail = tail * pulled[:, lanes]
            g = inside + pull_tail
            dproj_ref[rows, cols.u + LANES * p : cols.u + LANES * (p + 1)] = (
                dt_w * g + dsk_ref[0:1, lanes] * dy
            ).astype(B16)
            dy_fade = dy * fade
            dy_fades.append(dy_fade.astype(B16))
            u_tails.append((u * dt_w * tail).astype(B16))
            fades.append(jnp.exp(end))
            carry_terms.append((dy_fade * carried[:, lanes]).astype(B16))
            direct_terms.append((u * g).astype(B16))
            tail_terms.append((u * pull_tail).astype(B16))
        dy_fade = jnp.concatenate(dy_fades, axis=1)
        dcb = jnp.where(upper, dcb, 0.0).astype(B16)
        dproj_ref[rows, cols.c : cols.c + LANES] = (tn(dcb, bm) + nt(dy_fade, low_state)).astype(B16)
        dproj_ref[rows, cols.b : cols.b + LANES] = (
            nn(dcb, cm) + nt(jnp.concatenate(u_tails, axis=1), low_grad)
        ).astype(B16)
        group = group_ref[...]
        carry_term = nn(jnp.concatenate(carry_terms, axis=1), group)
        direct_term = nn(jnp.concatenate(direct_terms, axis=1), group)
        tail_term = dt * nn(jnp.concatenate(tail_terms, axis=1), group)
        overlap = jnp.sum(low_state.astype(F32) * grads_out, axis=0, keepdims=True)
        overlap = exact(jnp.broadcast_to(overlap, (8, width)), group.astype(F32))[0:1, :]
        overlap = overlap * jnp.exp(run[STEP - 1 : STEP, :])
        row_sum = jnp.concatenate(row_sums + [zero_rows], axis=0).T
        d_run = row_sum - col_sums + carry_term - tail_term
        d_a = exact(triu, d_run) + (jnp.sum(tail_term, axis=0, keepdims=True) + overlap)
        d_step = (direct_term - decay * d_a) * sigmoid(raw)
        dproj_ref[rows, cols.step : cols.step + LANES] = d_step.astype(B16)
        heads_ref[0:1, :] += jnp.sum(d_a * a, axis=0, keepdims=True)
        heads_ref[1:2, :] += jnp.sum(d_step, axis=0, keepdims=True)
        grad_state[...] = grads_out * jnp.concatenate(fades, axis=1) + tn(cm, dy_fade)
        return 0

    lax.fori_loop(0, blocks, scan_block, 0)
    skip = jnp.sum(skip_sum[...], axis=0, keepdims=True)
    heads_ref[2:3, :] = exact(jnp.broadcast_to(skip, (8, width)), group_ref[...].astype(F32))[0:1, :]
    multiply_back(dproj_ref, wcat_ref, part_ref)


def multiply_back(grad_ref, weight_ref, part_ref):
    def out_rows(i, _):
        rows = pl.ds(pl.multiple_of(i * TILE, TILE), TILE)
        block = grad_ref[rows, :]
        for first in range(0, weight_ref.shape[0], 256):
            part_ref[rows, first : first + 256] = nt(
                block, weight_ref[first : first + 256, :]
            ).astype(B16)
        return 0

    lax.fori_loop(0, grad_ref.shape[0] // TILE, out_rows, 0)


def ffn_fwd_kernel(rows_ref, wgu_ref, wdown_ref, gu_ref, hidden_ref, part_ref):
    units = hidden_ref.shape[1]

    def up(i, _):
        rows = pl.ds(pl.multiple_of(i * TILE, TILE), TILE)
        block = rows_ref[rows, :]
        g = nn(block, wgu_ref[:, :units])
        v = nn(block, wgu_ref[:, units:])
        gu_ref[rows, :units] = g.astype(B16)
        gu_ref[rows, units:] = v.astype(B16)
        hidden_ref[rows, :] = (g * sigmoid(g) * v).astype(B16)
        return 0

    lax.fori_loop(0, rows_ref.shape[0] // TILE, up, 0)
    multiply_out(hidden_ref, wdown_ref, part_ref)


def ffn_bwd_kernel(out_ref, wgu_ref, wdown_ref, gu_ref, dgu_ref, part_ref):
    ways, units, piece = wdown_ref.shape

    def down(i, _):
        rows = pl.ds(pl.multiple_of(i * TILE, TILE), TILE)
        dh = nt(out_ref[rows, 0:piece], wdown_ref[0])
        for k in range(1, ways):
            dh += nt(out_ref[rows, k * piece : (k + 1) * piece], wdown_ref[k])
        g = gu_ref[rows, :units].astype(F32)
        v = gu_ref[rows, units:].astype(F32)
        sg = sigmoid(g)
        dgu_ref[rows, :units] = (dh * v * sg * (1.0 + g * (1.0 - sg))).astype(B16)
        dgu_ref[rows, units:] = (dh * g * sg).astype(B16)
        return 0

    lax.fori_loop(0, out_ref.shape[0] // TILE, down, 0)
    multiply_back(dgu_ref, wgu_ref, part_ref)


def whole_call(kernel, outs, scratch, flops, name):
    vmem = pl.BlockSpec(memory_space=pltpu.VMEM)

    def call(*operands):
        moved = sum(o.size * o.dtype.itemsize for o in operands)
        return pl.pallas_call(
            kernel,
            out_shape=[jax.ShapeDtypeStruct(s, t) for s, t in outs],
            in_specs=[vmem] * len(operands),
            out_specs=[vmem] * len(outs),
            scratch_shapes=scratch,
            compiler_params=pltpu.CompilerParams(vmem_limit_bytes=VMEM_LIMIT),
            cost_estimate=pl.CostEstimate(flops=flops, bytes_accessed=2 * moved, transcendentals=0),
            name=name,
        )(*operands)

    return call


def core_fwd(cols, rows, wcat, wout, hp, dsk):
    length, depth = rows.shape
    width = cols.width
    return whole_call(
        functools.partial(core_fwd_kernel, cols),
        [
            ((length, cols.step), B16),
            ((length, LANES), F32),
            ((length, width), B16),
            ((length, width + LANES), B16),
            ((length // STEP, NS, width), B16),
            ((length // TILE, 8, 2 * TILE), F32),
            ((length, depth), B16),
        ],
        [pltpu.VMEM((NS, width), F32)],
        20 * length * depth * cols.total,
        "core_fwd",
    )(rows, wcat, wout, hp, dsk)


def core_bwd(cols, back, wcat, wout, hp, dsk, group, kept):
    length, depth = back.shape
    width = cols.width
    return whole_call(
        functools.partial(core_bwd_kernel, cols),
        [((length, cols.total), B16), ((8, LANES), F32), ((length, depth), B16)],
        [
            pltpu.VMEM((length, width + LANES), B16),
            pltpu.VMEM((NS, width), F32),
            pltpu.VMEM((STEP, width), F32),
            pltpu.VMEM((length, LANES), F32),
            pltpu.VMEM((length, LANES), F32),
        ],
        40 * length * depth * cols.total,
        "core_bwd",
    )(back, wcat, wout, hp, dsk, group, *kept)


def ffn_fwd(rows, wgu, wdown):
    length, depth = rows.shape
    units = wdown.shape[1]
    return whole_call(
        ffn_fwd_kernel,
        [((length, 2 * units), B16), ((length, units), B16), ((length, depth), B16)],
        [],
        6 * length * depth * units,
        "ffn_fwd",
    )(rows, wgu, wdown)


def ffn_bwd(out, wgu, wdown, gu):
    length, depth = out.shape
    units = wdown.shape[1]
    return whole_call(
        ffn_bwd_kernel,
        [((length, 2 * units), B16), ((length, depth), B16)],
        [],
        6 * length * depth * units,
        "ffn_bwd",
    )(out, wgu, wdown, gu)


def widen(block, axis, size):
    missing = size - block.shape[axis]
    if missing == 0:
        return block
    pads = [(0, 0)] * block.ndim
    pads[axis] = (0, missing)
    return jnp.pad(block, pads)


def rms(rows, gain):
    scale = lax.rsqrt(jnp.mean(rows * rows, axis=-1, keepdims=True) + EPS)
    return rows * scale * gain


def rms_back(rows, gain, grad):
    scale = lax.rsqrt(jnp.mean(rows * rows, axis=-1, keepdims=True) + EPS)
    scaled = gain * grad
    mean = jnp.mean(scaled * rows, axis=-1, keepdims=True)
    return scale * scaled - rows * (scale * scale * scale * mean), jnp.sum(
        grad * rows * scale, axis=0
    )


def gather_rows(block):
    return lax.all_gather(block, "tensor", axis=0, tiled=True)


def scatter_rows(block):
    return lax.psum_scatter(block, "tensor", scatter_dimension=0, tiled=True).astype(F32)


def on_device(
    acts_in, out_grad, mix_gain, w_mixer_in, w_query, w_shared, w_step, a_log, dt_bias, d_skip,
    w_mamba_out, w_attn_out, ffn_gain, w_gate_up, w_down,
):
    section = lax.axis_index("pipe")
    member = lax.axis_index("tensor")
    dp = lax.axis_size("dp")
    heads = a_log.shape[1]
    even = heads + heads % 2
    real = heads * HD
    width = even * HD
    q_real = w_query.shape[2]
    group = member * (q_real // HD) // (HA // KVH)
    cols = Cols(width)
    units = w_gate_up.shape[3]
    depth = acts_in.shape[2]
    piece = depth // dp

    shared = w_shared[0]
    keys = lax.dynamic_slice_in_dim(shared, 2 * NS + group * HD, HD, 1)
    values = lax.dynamic_slice_in_dim(shared, 2 * NS + KVH * HD + group * HD, HD, 1)
    steps = lax.dynamic_slice_in_dim(w_step[0], member * heads, heads, 1)
    wcat = jnp.concatenate(
        [
            widen(w_mixer_in[0, :, 0], 1, width),
            widen(w_mixer_in[0, :, 1], 1, width),
            widen(w_query[0], 1, LANES),
            shared[:, : 2 * NS],
            keys, keys, values, values,
            widen(steps, 1, LANES),
        ],
        axis=1,
    )
    gates = w_gate_up[0].reshape(piece, 2 * units)
    wout = jnp.concatenate(
        [
            widen(w_mamba_out[0], 0, width),
            widen(w_attn_out[0], 0, LANES),
            w_down[0],
            widen(jnp.concatenate([mix_gain, ffn_gain]), 0, 16),
        ],
        axis=0,
    )
    both = ("pipe", "dp")
    wcat_all = lax.all_gather(wcat, both, axis=0, tiled=True).reshape(2, depth, cols.total)
    wout_all = lax.all_gather(wout, both, axis=0)
    gates_all = lax.all_gather(gates, both, axis=0, tiled=True).reshape(2, depth, 2 * units)
    wout_all = wout_all.reshape((2, dp) + wout.shape)
    heads_all = lax.all_gather(jnp.concatenate([a_log, dt_bias, d_skip]), "pipe", axis=0)

    core_rows = width + LANES
    sub = jnp.arange(width)[:, None] // HD == jnp.arange(LANES)[None, :]
    layers = []
    for layer in range(2):
        gains = wout_all[layer, :, core_rows + units : core_rows + units + 2]
        gains = gains.transpose(1, 0, 2).reshape(2, depth).astype(F32)
        hp = widen(widen(heads_all[layer], 1, LANES), 0, 8)
        layers.append(
            dict(
                wcat=wcat_all[layer],
                wout=wout_all[layer, :, :core_rows],
                wdown=wout_all[layer, :, core_rows : core_rows + units],
                wgu=gates_all[layer],
                gains=gains,
                hp=hp,
                dsk=jnp.broadcast_to(jnp.repeat(hp[2, :even], HD)[None], (8, width)),
                group=sub.astype(B16),
            )
        )

    x = lax.dynamic_index_in_dim(acts_in, section, 0, False).astype(F32)
    y_grad = lax.dynamic_index_in_dim(out_grad, section, 0, False)
    kept = []
    for w in layers:
        rows_mix = gather_rows(rms(x, w["gains"][0]).astype(B16))
        *saved, part = core_fwd(cols, rows_mix, w["wcat"], w["wout"], w["hp"], w["dsk"])
        residual = x + scatter_rows(part)
        rows_ffn = gather_rows(rms(residual, w["gains"][1]).astype(B16))
        gu, hidden, part = ffn_fwd(rows_ffn, w["wgu"], w["wdown"])
        out = (residual + scatter_rows(part)).astype(B16)
        kept.append((x, rows_mix, saved, residual, rows_ffn, gu, hidden, out))
        x = out.astype(F32)

    x_grads, grads = [None, None], [None, None]
    for layer in (1, 0):
        w = layers[layer]
        x, rows_mix, saved, residual, rows_ffn, gu, hidden, _ = kept[layer]
        rows_out = gather_rows(y_grad)
        dgu, part = ffn_bwd(rows_out, w["wgu"], w["wdown"], gu)
        step_back, gain_ffn = rms_back(residual, w["gains"][1], scatter_rows(part))
        d_residual = y_grad.astype(F32) + step_back
        rows_back = gather_rows(d_residual.astype(B16))
        dproj, head_grads, part = core_bwd(
            cols, rows_back, w["wcat"], w["wout"], w["hp"], w["dsk"], w["group"], saved
        )
        step_back, gain_mix = rms_back(x, w["gains"][0], scatter_rows(part))
        y_grad = (d_residual + step_back).astype(B16)
        x_grads[layer] = y_grad
        g_gu = tn(rows_ffn, dgu).astype(B16)
        g_cat = tn(rows_mix, dproj).astype(B16)
        lows = saved[3]
        by_piece = lambda rows: rows.reshape(rows.shape[0], dp, piece)
        g_down = jnp.einsum("lf,lkd->kfd", hidden, by_piece(rows_out), preferred_element_type=F32)
        g_out = jnp.einsum("lf,lkd->kfd", lows, by_piece(rows_back), preferred_element_type=F32)
        g_rows = jnp.concatenate([g_out, g_down], axis=1).astype(B16)
        g_cols = jnp.concatenate([g_cat[:, : cols.b], g_gu], axis=1)
        g_kv = g_cat[:, cols.k : cols.k + 2 * LANES].astype(F32).reshape(depth, 2, 2, HD).sum(2)
        g_kv = lax.dynamic_update_slice(
            jnp.zeros((depth, 2, KVH, HD), F32), g_kv[:, :, None, :], (0, 0, group, 0)
        )
        g_step = lax.dynamic_update_slice_in_dim(
            jnp.zeros((depth, LANES), F32),
            g_cat[:, cols.step : cols.step + heads].astype(F32), member * heads, 1,
        )
        g_shared = jnp.concatenate(
            [g_cat[:, cols.b : cols.k].astype(F32), g_kv.reshape(depth, -1), g_step], axis=1
        ).astype(B16)
        small = jnp.concatenate([gain_mix, gain_ffn])
        grads[layer] = (
            lax.psum_scatter(g_cols, "dp", scatter_dimension=0, tiled=True),
            lax.psum_scatter(g_rows, "dp", scatter_dimension=0, tiled=False),
            lax.psum_scatter(g_shared, ("dp", "tensor"), scatter_dimension=0, tiled=True),
            small,
            head_grads[:3, :heads],
        )

    def swap(own, other):
        return lax.ppermute(jnp.where(section == 0, other, own), "pipe", [(0, 1), (1, 0)])

    def pick(pair):
        return jnp.where(section == 0, pair[0], pair[1])

    def placed(pair):
        mine, received = pick(pair), swap(*pair)
        return jnp.where(
            section == 0, jnp.stack([mine, received]), jnp.stack([received, mine])
        )

    acts = placed([k[-1] for k in kept])
    in_grads = placed(x_grads)
    totals = [
        pick(pair).astype(F32) + swap(*pair).astype(F32)
        for pair in zip(grads[0][:3], grads[1][:3])
    ]
    small = jnp.stack([g[3] for g in grads]).reshape(2, 2, depth)
    small = lax.psum(lax.psum_scatter(small, ("dp", "tensor"), scatter_dimension=2, tiled=True), "pipe")
    head_sum = lax.psum(jnp.stack([g[4] for g in grads]), both)
    g_cols, g_rows, g_shared = totals
    g_mixer = jnp.stack([g_cols[:, :real], g_cols[:, width : width + real]], axis=1)
    g_gates = g_cols[:, cols.b :].reshape(piece, 2, units)
    return (
        acts[None],
        in_grads[None],
        pick(small)[None],
        g_mixer[None],
        g_cols[None, :, cols.q : cols.q + q_real],
        g_shared[None, :, : 2 * NS + 2 * KVH * HD],
        g_shared[None, :, 2 * NS + 2 * KVH * HD :][:, :, :HM],
        pick(head_sum)[None],
        g_rows[None, :real],
        g_rows[None, width : width + q_real],
        g_gates[None],
        g_rows[None, core_rows:],
    )


def solution(mesh):
    placed = (
        P("dp", "tensor", None),
        P("dp", "tensor", None),
        P("pipe", "dp"),
        P("pipe", "dp", None, "tensor"),
        P("pipe", "dp", "tensor"),
        P("pipe", "dp", None),
        P("pipe", "dp", None),
        P("pipe", "tensor"),
        P("pipe", "tensor"),
        P("pipe", "tensor"),
        P("pipe", "tensor", "dp"),
        P("pipe", "tensor", "dp"),
        P("pipe", "dp"),
        P("pipe", "dp", None, "tensor"),
        P("pipe", "tensor", "dp"),
    )
    return jax.shard_map(
        on_device,
        mesh=mesh,
        in_specs=placed,
        out_specs=(
            P("pipe", "dp", "tensor", None),
            P("pipe", "dp", "tensor", None),
            P("pipe", None, ("dp", "tensor")),
            P("pipe", "dp", None, "tensor"),
            P("pipe", "dp", "tensor"),
            P("pipe", ("dp", "tensor"), None),
            P("pipe", ("dp", "tensor"), None),
            P("pipe", None, "tensor"),
            P("pipe", "tensor", "dp"),
            P("pipe", "tensor", "dp"),
            P("pipe", "dp", None, "tensor"),
            P("pipe", "tensor", "dp"),
        ),
        check_vma=False,
    )
```

profile of v0, /device:TPU:8, one launch (start us, length us, event | category | flops | bytes accessed | tf_op | source)
XLA Modules:
  0.0 1311.8 jit_solution(14234595809949935992)
XLA Ops:
  13.3 72.1 %all-gather.34.cloned.1.call-done = bf16[8320,256]{1,0:T(8,128)(2,1)} async-done(((bf16[1040,256]{1,0:T(8,128)(2,1)}), bf16[8320,256]{1,0:T(8,128)(2,1)}) %all-gather.34.cloned.1.call-update) | async-done | bytes 4259856 | tf_op jit(solution)/shard_map/all_gather | solution.py:598
  96.8 87.9 %all-gather.18.cloned.1.call-done = bf16[2048,1536]{1,0:T(8,128)(2,1)} async-done(((bf16[256,1536]{1,0:T(8,128)(2,1)}), bf16[2048,1536]{1,0:T(8,128)(2,1)}) %all-gather.18.cloned.1.call-update) | async-done | bytes 6291472 | tf_op jit(solution)/shard_map/all_gather | solution.py:597
  190.6 18.5 %all-gather.16.cloned.1.call-done.rows_ref = bf16[1024,1024]{1,0:T(8,128)(2,1)} async-done(((bf16[256,1024]{1,0:T(8,128)(2,1)}), bf16[1024,1024]{1,0:T(8,128)(2,1)}) %all-gather.16.cloned.1.call-update) | async-done | bytes 2097168 | tf_op jit(solution)/shard_map/all_gather | solution.py:546
  209.6 22.2 %core_fwd.2 = (bf16[1024,1408]{1,0:T(8,128)(2,1)}, f32[1024,128]{1,0:T(8,128)}, bf16[1024,384]{1,0:T(8,128)(2,1)}, bf16[1024,512]{1,0:T(8,128)(2,1)}, bf16[8,128...) custom-call(bf16[1024,1024]{1,0:T(8,128)(2,1)} %all-gather.16.cloned.1.call-done.rows_ref, ...), custom_call_target="tpu_custom_call" | custom-call | flops 32212254720 | bytes 12615680 | tf_op jit(solution)/shard_map/core_fwd/pallas_call | solution.py:446
  233.8 29.6 %reduce-scatter.18.cloned.1.call-done = bf16[256,1024]{1,0:T(8,128)(2,1)} async-done(((bf16[1024,1024]{1,0:T(8,128)(2,1)}), bf16[256,1024]{1,0:T(8,128)(2,1)}) %reduce-scatter.18.cloned.1.call-update) | async-done | bytes 524304 | tf_op jit(solution)/shard_map/reduce_scatter | solution.py:550
  266.9 71.5 %all-gather.22.cloned.1.call-done = bf16[2048,1024]{1,0:T(8,128)(2,1)} async-done(((bf16[256,1024]{1,0:T(8,128)(2,1)}), bf16[2048,1024]{1,0:T(8,128)(2,1)}) %all-gather.22.cloned.1.call-update) | async-done | bytes 4194320 | tf_op jit(solution)/shard_map/all_gather | solution.py:599
  343.0 18.4 %all-gather.20.cloned.1.call-done.rows_ref = bf16[1024,1024]{1,0:T(8,128)(2,1)} async-done(((bf16[256,1024]{1,0:T(8,128)(2,1)}), bf16[1024,1024]{1,0:T(8,128)(2,1)}) %all-gather.20.cloned.1.call-update) | async-done | bytes 2097168 | tf_op jit(solution)/shard_map/all_gather | solution.py:546
  370.5 31.5 %reduce-scatter.20.cloned.1.call-done = bf16[256,1024]{1,0:T(8,128)(2,1)} async-done(((bf16[1024,1024]{1,0:T(8,128)(2,1)}), bf16[256,1024]{1,0:T(8,128)(2,1)}) %reduce-scatter.20.cloned.1.call-update) | async-done | bytes 524304 | tf_op jit(solution)/shard_map/reduce_scatter | solution.py:550
  405.2 21.9 %all-gather.24.cloned.1.call-done.rows_ref = bf16[1024,1024]{1,0:T(8,128)(2,1)} async-done(((bf16[256,1024]{1,0:T(8,128)(2,1)}), bf16[1024,1024]{1,0:T(8,128)(2,1)}) %all-gather.24.cloned.1.call-update) | async-done | bytes 2097168 | tf_op jit(solution)/shard_map/all_gather | solution.py:546
  427.8 22.1 %core_fwd.3 = (bf16[1024,1408]{1,0:T(8,128)(2,1)}, f32[1024,128]{1,0:T(8,128)}, bf16[1024,384]{1,0:T(8,128)(2,1)}, bf16[1024,512]{1,0:T(8,128)(2,1)}, bf16[8,128...) custom-call(bf16[1024,1024]{1,0:T(8,128)(2,1)} %all-gather.24.cloned.1.call-done.rows_ref, ...), custom_call_target="tpu_custom_call" | custom-call | flops 32212254720 | bytes 12615680 | tf_op jit(solution)/shard_map/core_fwd/pallas_call | solution.py:446
  450.0 31.5 %reduce-scatter.22.cloned.1.call-done = bf16[256,1024]{1,0:T(8,128)(2,1)} async-done(((bf16[1024,1024]{1,0:T(8,128)(2,1)}), bf16[256,1024]{1,0:T(8,128)(2,1)}) %reduce-scatter.22.cloned.1.call-update) | async-done | bytes 524304 | tf_op jit(solution)/shard_map/reduce_scatter | solution.py:550
  486.3 21.3 %all-gather.26.cloned.1.call-done.rows_ref = bf16[1024,1024]{1,0:T(8,128)(2,1)} async-done(((bf16[256,1024]{1,0:T(8,128)(2,1)}), bf16[1024,1024]{1,0:T(8,128)(2,1)}) %all-gather.26.cloned.1.call-update) | async-done | bytes 2097168 | tf_op jit(solution)/shard_map/all_gather | solution.py:546
  516.7 15.2 %all-gather.36.cloned.1.call-done = bf16[1,1024,1024]{2,1,0:T(8,128)(2,1)} async-done(((bf16[1,256,1024]{2,1,0:T(8,128)(2,1)}), bf16[1,1024,1024]{2,1,0:T(8,128)(2,1)}) %all-gather.36.cloned.1.call-update) | async-done | bytes 2097168 | tf_op jit(solution)/shard_map/all_gather | solution.py:546
  531.9 9.9 ffn_bwd.2
  541.9 31.5 %reduce-scatter.26.cloned.1.call-done = bf16[256,1024]{1,0:T(8,128)(2,1)} async-done(((bf16[1024,1024]{1,0:T(8,128)(2,1)}), bf16[256,1024]{1,0:T(8,128)(2,1)}) %reduce-scatter.26.cloned.1.call-update) | async-done | bytes 524304 | tf_op jit(solution)/shard_map/reduce_scatter | solution.py:550
  578.7 21.9 %all-gather.28.cloned.1.call-done.back_ref = bf16[1024,1024]{1,0:T(8,128)(2,1)} async-done(((bf16[256,1024]{1,0:T(8,128)(2,1)}), bf16[1024,1024]{1,0:T(8,128)(2,1)}) %all-gather.28.cloned.1.call-update) | async-done | bytes 2097168 | tf_op jit(solution)/shard_map/all_gather | solution.py:546
  600.6 29.0 %core_bwd.2 = (bf16[1024,1536]{1,0:T(8,128)(2,1)}, f32[8,128]{1,0:T(8,128)}, bf16[1024,1024]{1,0:T(8,128)(2,1)}) custom-call(bf16[1024,1024]{1,0:T(8,128)(2,1)} %all-gather.28.cloned.1.call-done.back_ref, bf16[1024,1536]{1,0:T(8,128)(2,1)} %get-tuple-element.120.wcat_ref, bf16[4,512,256]{2,1,0:T(8,128)(2,1)} %get-tuple-element.123.wout_ref, ...), custom_call_target="tpu_custom_call" | custom-call | flops 64424509440 | bytes 25001984 | tf_op jit(solution)/shard_map/core_bwd/pallas_call | solution.py:446
  629.7 31.5 %reduce-scatter.28.cloned.1.call-done = bf16[256,1024]{1,0:T(8,128)(2,1)} async-done(((bf16[1024,1024]{1,0:T(8,128)(2,1)}), bf16[256,1024]{1,0:T(8,128)(2,1)}) %reduce-scatter.28.cloned.1.call-update) | async-done | bytes 524304 | tf_op jit(solution)/shard_map/reduce_scatter | solution.py:550
  665.4 22.7 %all-gather.30.cloned.1.call-done.out_ref = bf16[1024,1024]{1,0:T(8,128)(2,1)} async-done(((bf16[256,1024]{1,0:T(8,128)(2,1)}), bf16[1024,1024]{1,0:T(8,128)(2,1)}) %all-gather.30.cloned.1.call-update) | async-done | bytes 2097168 | tf_op jit(solution)/shard_map/all_gather | solution.py:546
  688.1 9.9 ffn_bwd.3
  698.1 31.5 %reduce-scatter.30.cloned.1.call-done = bf16[256,1024]{1,0:T(8,128)(2,1)} async-done(((bf16[1024,1024]{1,0:T(8,128)(2,1)}), bf16[256,1024]{1,0:T(8,128)(2,1)}) %reduce-scatter.30.cloned.1.call-update) | async-done | bytes 524304 | tf_op jit(solution)/shard_map/reduce_scatter | solution.py:550
  733.6 22.5 %all-gather.32.cloned.1.call-done.back_ref = bf16[1024,1024]{1,0:T(8,128)(2,1)} async-done(((bf16[256,1024]{1,0:T(8,128)(2,1)}), bf16[1024,1024]{1,0:T(8,128)(2,1)}) %all-gather.32.cloned.1.call-update) | async-done | bytes 2097168 | tf_op jit(solution)/shard_map/all_gather | solution.py:546
  756.1 29.0 %core_bwd.3 = (bf16[1024,1536]{1,0:T(8,128)(2,1)}, f32[8,128]{1,0:T(8,128)}, bf16[1024,1024]{1,0:T(8,128)(2,1)}) custom-call(bf16[1024,1024]{1,0:T(8,128)(2,1)} %all-gather.32.cloned.1.call-done.back_ref, bf16[1024,1536]{1,0:T(8,128)(2,1)} %get-tuple-element.121.wcat_ref, bf16[4,512,256]{2,1,0:T(8,128)(2,1)} %get-tuple-element.125.wout_ref, ...), custom_call_target="tpu_custom_call" | custom-call | flops 64424509440 | bytes 25001984 | tf_op jit(solution)/shard_map/core_bwd/pallas_call | solution.py:446
  903.8 13.2 %collective-permute-done = bf16[256,1024]{1,0:T(8,128)(2,1)S(1)} collective-permute-done((bf16[256,1024]{1,0:T(8,128)(2,1)S(1)}, bf16[256,1024]{1,0:T(8,128)(2,1)S(1)}, u32[]{:S(2)}, u32[]{:S(2)}) %collective-permute-start) | collective-permute-done | bytes 524320 | tf_op jit(solution)/shard_map/ppermute | solution.py:680
  918.1 17.8 %psum.15 = f32[2,3,6]{2,1,0:T(4,128)S(1)} all-reduce(f32[2,3,6]{2,1,0:T(4,128)S(1)} %pad_maximum_fusion.10), channel_id=1, replica_groups=mesh['pipe'=2,'dp'=4,'tensor'=4] {'pipe','dp'}, use_global_device_ids=true, to_apply=%region_28.29 | all-reduce | flops 36 | bytes 288 | tf_op jit(solution)/shard_map/psum | solution.py:699
  935.9 38.3 %reduce-scatter.38.cloned.1.call-done = bf16[64,640]{1,0:T(8,128)(2,1)} async-done(((bf16[1024,640]{1,0:T(8,128)(2,1)}), bf16[64,640]{1,0:T(8,128)(2,1)}) %reduce-scatter.38.cloned.1.call-update) | async-done | bytes 81936 | tf_op jit(solution)/shard_map/reduce_scatter | solution.py:674
  985.9 31.2 %reduce-scatter.44.cloned.1.call-done = bf16[1,1024,256]{1,2,0:T(8,128)(2,1)} async-done(((bf16[4,1024,256]{1,2,0:T(8,128)(2,1)}), bf16[1,1024,256]{1,2,0:T(8,128)(2,1)}) %reduce-scatter.44.cloned.1.call-update) | async-done | bytes 524304 | tf_op jit(solution)/shard_map/reduce_scatter | solution.py:673
  1017.2 45.6 %reduce-scatter.42.cloned.1.call-done = bf16[1,1024,256]{1,2,0:T(8,128)(2,1)} async-done(((bf16[4,1024,256]{1,2,0:T(8,128)(2,1)}), bf16[1,1024,256]{1,2,0:T(8,128)(2,1)}) %reduce-scatter.42.cloned.1.call-update) | async-done | bytes 524304 | tf_op jit(solution)/shard_map/reduce_scatter | solution.py:673
  1065.5 58.5 %reduce-scatter.46.cloned.1.call-done = f32[64,4]{1,0:T(8,128)} async-done(((f32[1024,4]{1,0:T(8,128)}), f32[64,4]{1,0:T(8,128)}) %reduce-scatter.46.cloned.1.call-update) | async-done | bytes 1040
  1130.5 67.7 %reduce-scatter.36.cloned.1.call-done = bf16[256,1920]{0,1:T(8,128)(2,1)} async-done(((bf16[1024,1920]{0,1:T(8,128)(2,1)}), bf16[256,1920]{0,1:T(8,128)(2,1)}) %reduce-scatter.36.cloned.1.call-update) | async-done | bytes 983056 | tf_op jit(solution)/shard_map/reduce_scatter | solution.py:672
  1198.1 75.3 %reduce-scatter.34.cloned.1.call-done = bf16[256,1920]{0,1:T(8,128)(2,1)} async-done(((bf16[1024,1920]{0,1:T(8,128)(2,1)}), bf16[256,1920]{0,1:T(8,128)(2,1)}) %reduce-scatter.34.cloned.1.call-update) | async-done | bytes 983056 | tf_op jit(solution)/shard_map/reduce_scatter | solution.py:672
  1282.6 17.0 %collective-permute-done.2 = bf16[256,1920]{0,1:T(8,128)(2,1)} collective-permute-done((bf16[256,1920]{0,1:T(8,128)(2,1)}, bf16[256,1920]{0,1:T(8,128)(2,1)}, u32[]{:S(2)}, u32[]{:S(2)}) %collective-permute-start.2) | collective-permute-done | bytes 983072 | tf_op jit(solution)/shard_map/ppermute | solution.py:680
  (274 shorter events, 228.5 us)
Async XLA Ops:
  7.2 78.2 %all-gather.34.cloned.1.call-start = ((), (), s32[]{:S(2)}) async-start(), calls=%async_computation.38 | async-start | bytes 4792320 | tf_op jit(solution)/shard_map/all_gather | solution.py:598
  9.9 174.7 %all-gather.18.cloned.1.call-start = ((), (), s32[]{:S(2)}) async-start(), calls=%async_computation.16 | async-start | bytes 7077888 | tf_op jit(solution)/shard_map/all_gather | solution.py:597
  13.1 196.0 %all-gather.16.cloned.1.call-start = ((), (), s32[]{:S(2)}) async-start(), calls=%async_computation.15 | async-start | bytes 2621440 | tf_op jit(solution)/shard_map/all_gather | solution.py:546
  87.2 176.2 %reduce-scatter.18.cloned.1.call-start = ((), (), s32[]{:S(2)}) async-start(), calls=%async_computation.17 | async-start | bytes 2621440 | tf_op jit(solution)/shard_map/reduce_scatter | solution.py:550
  231.8 106.5 %all-gather.22.cloned.1.call-start = ((), (), s32[]{:S(2)}) async-start(), calls=%async_computation.19 | async-start | bytes 4718592 | tf_op jit(solution)/shard_map/all_gather | solution.py:599
  233.8 127.6 %all-gather.20.cloned.1.call-start = ((), (), s32[]{:S(2)}) async-start(), calls=%async_computation.18 | async-start | bytes 2621440 | tf_op jit(solution)/shard_map/all_gather | solution.py:546
  266.8 135.2 %reduce-scatter.20.cloned.1.call-start = ((), (), s32[]{:S(2)}) async-start(), calls=%async_computation.20 | async-start | bytes 2621440 | tf_op jit(solution)/shard_map/reduce_scatter | solution.py:550
  370.4 56.7 %all-gather.24.cloned.1.call-start = ((), (), s32[]{:S(2)}) async-start(), calls=%async_computation.21 | async-start | bytes 2621440 | tf_op jit(solution)/shard_map/all_gather | solution.py:546
  404.4 77.1 %reduce-scatter.22.cloned.1.call-start = ((), (), s32[]{:S(2)}) async-start(), calls=%async_computation.22 | async-start | bytes 2621440 | tf_op jit(solution)/shard_map/reduce_scatter | solution.py:550
  449.9 57.7 %all-gather.26.cloned.1.call-start = ((), (), s32[]{:S(2)}) async-start(), calls=%async_computation.23 | async-start | bytes 2621440 | tf_op jit(solution)/shard_map/all_gather | solution.py:546
  484.9 47.0 %all-gather.36.cloned.1.call-start = ((), (), s32[]{:S(2)}) async-start(), calls=%async_computation.39 | async-start | bytes 2621440 | tf_op jit(solution)/shard_map/all_gather | solution.py:546
  485.8 87.7 %reduce-scatter.26.cloned.1.call-start = ((), (), s32[]{:S(2)}) async-start(), calls=%async_computation.25 | async-start | bytes 2621440 | tf_op jit(solution)/shard_map/reduce_scatter | solution.py:550
  541.9 58.8 %all-gather.28.cloned.1.call-start = ((), (), s32[]{:S(2)}) async-start(), calls=%async_computation.26 | async-start | bytes 2621440 | tf_op jit(solution)/shard_map/all_gather | solution.py:546
  577.9 83.3 %reduce-scatter.28.cloned.1.call-start = ((), (), s32[]{:S(2)}) async-start(), calls=%async_computation.27 | async-start | bytes 2621440 | tf_op jit(solution)/shard_map/reduce_scatter | solution.py:550
  629.7 58.4 %all-gather.30.cloned.1.call-start = ((), (), s32[]{:S(2)}) async-start(), calls=%async_computation.28 | async-start | bytes 2621440 | tf_op jit(solution)/shard_map/all_gather | solution.py:546
  665.3 64.3 %reduce-scatter.30.cloned.1.call-start = ((), (), s32[]{:S(2)}) async-start(), calls=%async_computation.29 | async-start | bytes 2621440 | tf_op jit(solution)/shard_map/reduce_scatter | solution.py:550
  698.0 58.1 %all-gather.32.cloned.1.call-start = ((), (), s32[]{:S(2)}) async-start(), calls=%async_computation.30 | async-start | bytes 2621440 | tf_op jit(solution)/shard_map/all_gather | solution.py:546
  733.4 141.6 %reduce-scatter.32.cloned.1.call-start = ((), (), s32[]{:S(2)}) async-start(), calls=%async_computation.31 | async-start | bytes 2621440 | tf_op jit(solution)/shard_map/reduce_scatter | solution.py:550
  785.2 115.7 %reduce-scatter.24.cloned.1.call-start = ((), (), s32[]{:S(2)}) async-start(), calls=%async_computation.24 | async-start | bytes 2621440 | tf_op jit(solution)/shard_map/reduce_scatter | solution.py:550
  785.9 150.0 %reduce-scatter.40.cloned.1.call-start = ((), (), s32[]{:S(2)}) async-start(), calls=%async_computation.35 | async-start | bytes 1392640 | tf_op jit(solution)/shard_map/reduce_scatter | solution.py:674
  807.4 166.9 %reduce-scatter.38.cloned.1.call-start = ((), (), s32[]{:S(2)}) async-start(), calls=%async_computation.34 | async-start | bytes 1392640 | tf_op jit(solution)/shard_map/reduce_scatter | solution.py:674
  829.2 188.0 %reduce-scatter.44.cloned.1.call-start = ((), (), s32[]{:S(2)}) async-start(), calls=%async_computation.37 | async-start | bytes 2621440 | tf_op jit(solution)/shard_map/reduce_scatter | solution.py:673
  846.1 216.7 %reduce-scatter.42.cloned.1.call-start = ((), (), s32[]{:S(2)}) async-start(), calls=%async_computation.36 | async-start | bytes 2621440 | tf_op jit(solution)/shard_map/reduce_scatter | solution.py:673
  863.0 261.0 %reduce-scatter.46.cloned.1.call-start = ((), (), s32[]{:S(2)}) async-start(), calls=%async_computation.40 | async-start | bytes 557056
  880.4 317.8 %reduce-scatter.36.cloned.1.call-start = ((), (), s32[]{:S(2)}) async-start(), calls=%async_computation.33 | async-start | bytes 4915200 | tf_op jit(solution)/shard_map/reduce_scatter | solution.py:672
  885.0 388.5 %reduce-scatter.34.cloned.1.call-start = ((), (), s32[]{:S(2)}) async-start(), calls=%async_computation.32 | async-start | bytes 4915200 | tf_op jit(solution)/shard_map/reduce_scatter | solution.py:672
  902.3 14.7 %collective-permute-start = (bf16[256,1024]{1,0:T(8,128)(2,1)S(1)}, bf16[256,1024]{1,0:T(8,128)(2,1)S(1)}, u32[]{:S(2)}, u32[]{:S(2)}) collective-permute-start(bf16[256,1024]{1,0:T(8,128)(2,1)S(1)} %get-tuple-element.137), channel_id=1, source_target_pairs={{0,16},{16,0},{1,17},{17,1},{2,18},{18,2},{3,19},{19,3},{4,20},{20... | collective-permute-start | bytes 1572872 | tf_op jit(solution)/shard_map/ppermute | solution.py:680
  975.1 4.5 collective-permute-start.3
  984.5 295.7 %collective-permute-start.1 = (bf16[256,1024]{1,0:T(8,128)(2,1)}, bf16[256,1024]{1,0:T(8,128)(2,1)}, u32[]{:S(2)}, u32[]{:S(2)}) collective-permute-start(bf16[256,1024]{1,0:T(8,128)(2,1)} %broadcast_select_fusion.1), channel_id=1, source_target_pairs={{0,16},{16,0},{1,17},{17,1},{2,18},{18,2},{3,19},{19,3},{4,20},{20... | collective-permute-start | bytes 1572872 | tf_op jit(solution)/shard_map/ppermute | solution.py:680
  1017.2 260.0 %copy-start.16 = (bf16[1,1024,256]{1,2,0:T(8,128)(2,1)S(1)}, bf16[1,1024,256]{1,2,0:T(8,128)(2,1)}, u32[]{:S(2)}) copy-start(bf16[1,1024,256]{1,2,0:T(8,128)(2,1)} %reduce-scatter.44.cloned.1.call-done) | copy-start | bytes 1572868
  1064.0 213.2 %collective-permute-start.4 = (bf16[1024,256]{0,1:T(8,128)(2,1)S(1)}, bf16[1024,256]{0,1:T(8,128)(2,1)S(1)}, u32[]{:S(2)}, u32[]{:S(2)}) collective-permute-start(bf16[1024,256]{0,1:T(8,128)(2,1)S(1)} %select_bitcast_fusion), channel_id=1, source_target_pairs={{0,16},{16,0},{1,17},{17,1},{2,18},{18,2},{3,19},{19,3},{4,20},{20... | collective-permute-start | bytes 1572872 | tf_op jit(solution)/shard_map/ppermute | solution.py:680
  1275.7 23.8 %collective-permute-start.2 = (bf16[256,1920]{0,1:T(8,128)(2,1)}, bf16[256,1920]{0,1:T(8,128)(2,1)}, u32[]{:S(2)}, u32[]{:S(2)}) collective-permute-start(bf16[256,1920]{0,1:T(8,128)(2,1)} %broadcast_select_fusion), channel_id=1, source_target_pairs={{0,16},{16,0},{1,17},{17,1},{2,18},{18,2},{3,19},{19,3},{4,20},{20... | collective-permute-start | bytes 2949128 | tf_op jit(solution)/shard_map/ppermute | solution.py:680
  (35 other events, 1132.1 us)
Sparse Core Ops, SparseCore 0:
  10.7 74.6 all-gather.33
  88.1 96.5 all-gather.17
  186.8 22.1 all-gather.15
  232.0 31.4 reduce-scatter.17
  265.6 72.7 all-gather.21
  339.9 21.4 all-gather.19
  370.5 31.4 reduce-scatter.19
  404.5 22.5 all-gather.23
  450.0 31.4 reduce-scatter.21
  485.0 22.5 all-gather.25
  509.3 22.5 all-gather.35
  542.0 31.4 reduce-scatter.25
  578.0 22.5 all-gather.27
  629.8 31.4 reduce-scatter.27
  665.4 22.5 all-gather.29
  698.2 31.4 reduce-scatter.29
  733.5 22.5 all-gather.31
  785.3 31.3 reduce-scatter.31
  819.4 31.4 reduce-scatter.23
  854.3 58.2 reduce-scatter.39
  916.8 57.4 reduce-scatter.37
  976.5 40.6 reduce-scatter.43
  1019.6 43.1 reduce-scatter.41
  1066.8 57.1 reduce-scatter.45
  1126.4 71.6 reduce-scatter.35
  1200.4 73.0 reduce-scatter.33
where the time goes:
time: 1320 us; the launch traced here: 1310 us
  waiting for transfers between devices  932 us (71%)
  Pallas kernels  140 us (11%)
  local copies, waits for them, and re-layouts  83.3 us (6%)
  other arithmetic  65.7 us (5%)
  matrix products  39 us (3%)
  blocking collectives  27 us (2%)
  between operations  15.3 us (1%)
    reduce_scatter x8, waiting for transfers between devices, scatter_rows(): lax.psum_scatter(block, 'tensor', scatter_dimension=0, tiled=True)  187 us
    all_gather x8, waiting for transfers between devices, gather_rows(): return lax.all_gather(block, 'tensor', axis=0, tiled=True)  163 us
    reduce_scatter x2, waiting for transfers between devices, on_device(): lax.psum_scatter(g_cols, 'dp', scatter_dimension=0, tiled=True)  143 us
    pallas_call x8, Pallas kernels, call(): pl.pallas_call(kernel, out_shape=[jax.ShapeDtypeStruct(s, t) for s, t in...  140 us
    all_gather x1, waiting for transfers between devices, on_device(): lax.all_gather(wcat, both, axis=0, tiled=True).reshape(2, depth, cols.total)  87.9 us
    reduce_scatter x2, waiting for transfers between devices, on_device(): lax.psum_scatter(g_rows, 'dp', scatter_dimension=0, tiled=False)  76.9 us
    all_gather x1, waiting for transfers between devices, on_device(): wout_all = lax.all_gather(wout, both, axis=0)  72.1 us
    all_gather x1, waiting for transfers between devices, on_device(): lax.all_gather(gates, both, axis=0, tiled=True).reshape(2, depth, 2 * units)  71.5 us
  transfers between devices with their start and end apart: 31, of which 26 were waited for; matrix products, arithmetic and copies ran while one was open for 12% of the time, Pallas kernels for 1%

commit v1 on v0

--- a/solution.py
+++ b/solution.py
@@ -215,9 +215,9 @@
 
 
 def core_bwd_kernel(
-    cols, back_ref, wcat_ref, wout_ref, hp_ref, dsk_ref, group_ref, proj_ref, step_ref, y_ref, lows_ref,
-    states_ref, lse_ref,
-    dproj_ref, heads_ref, part_ref, dcore, grad_state, skip_sum, dk_sum, dv_sum,
+    cols, members, back_ref, wcat_ref, wout_ref, hp_ref, dsk_ref, group_ref, rows_ref, fold_ref,
+    proj_ref, step_ref, y_ref, lows_ref, states_ref, lse_ref,
+    dproj_ref, heads_ref, part_ref, dcore, grad_state, skip_sum, dk_sum, dv_sum, folded,
 ):
     length = back_ref.shape[0]
     width = cols.width
@@ -388,6 +388,22 @@
     heads_ref[2:3, :] = exact(jnp.broadcast_to(skip, (8, width)), group_ref[...].astype(F32))[0:1, :]
     multiply_back(dproj_ref, wcat_ref, part_ref)
 
+    def fold(i, _):
+        rows = pl.ds(pl.multiple_of(i * TILE, TILE), TILE)
+        folded[rows, :] = nn(dproj_ref[rows, cols.b :], fold_ref[...]).astype(B16)
+        return 0
+
+    lax.fori_loop(0, length // TILE, fold, 0)
+    depth = wcat_ref.shape[0]
+    share = depth // members
+    sub = piece // members
+    for k in range(ways):
+        grad = tn(rows_ref[:, k * piece : (k + 1) * piece], folded[...]).astype(B16)
+        for t in range(members):
+            part_ref[t * share + k * sub : t * share + (k + 1) * sub, depth:] = grad[
+                t * sub : (t + 1) * sub, :
+            ]
+
 
 def multiply_back(grad_ref, weight_ref, part_ref):
     def out_rows(i, _):
@@ -477,22 +493,24 @@
     )(rows, wcat, wout, hp, dsk)
 
 
-def core_bwd(cols, back, wcat, wout, hp, dsk, group, kept):
+def core_bwd(cols, members, back, wcat, wout, hp, dsk, group, rows, fold, kept):
     length, depth = back.shape
     width = cols.width
+    wide = cols.total - cols.b
     return whole_call(
-        functools.partial(core_bwd_kernel, cols),
-        [((length, cols.total), B16), ((8, LANES), F32), ((length, depth), B16)],
+        functools.partial(core_bwd_kernel, cols, members),
+        [((length, cols.total), B16), ((8, LANES), F32), ((length, depth + wide), B16)],
         [
             pltpu.VMEM((length, width + LANES), B16),
             pltpu.VMEM((NS, width), F32),
             pltpu.VMEM((STEP, width), F32),
             pltpu.VMEM((length, LANES), F32),
             pltpu.VMEM((length, LANES), F32),
+            pltpu.VMEM((length, wide), B16),
         ],
         40 * length * depth * cols.total,
         "core_bwd",
-    )(back, wcat, wout, hp, dsk, group, *kept)
+    )(back, wcat, wout, hp, dsk, group, rows, fold, *kept)
 
 
 def ffn_fwd(rows, wgu, wdown):
@@ -519,6 +537,307 @@
     )(out, wgu, wdown, gu)
 
 
+def grad_columns(rows_ref, grad_ref, out_ref):
+    _, ways, half, width = out_ref.shape
+    for k in range(ways):
+        block = rows_ref[:, 2 * half * k : 2 * half * (k + 1)]
+        for first in range(0, width, 512):
+            last = min(first + 512, width)
+            value = tn(block, grad_ref[:, first:last]).astype(B16)
+            out_ref[0, k, :, first:last] = value[:half, :]
+            out_ref[1, k, :, first:last] = value[half:, :]
+
+
+def grad_rows(lows_ref, back_ref, out_ref):
+    _, ways, half, piece = out_ref.shape
+    for h in range(2):
+        block = lows_ref[:, h * half : (h + 1) * half]
+        for k in range(ways):
+            out_ref[h, k] = tn(block, back_ref[:, k * piece : (k + 1) * piece]).astype(B16)
+
+
+def ffn_grads_kernel(rows_ref, dgu_ref, hidden_ref, out_ref, gu_ref, down_ref):
+    grad_columns(rows_ref, dgu_ref, gu_ref)
+    grad_rows(hidden_ref, out_ref, down_ref)
+
+
+def ffn_grads(ways, rows, dgu, hidden, out):
+    length, depth = rows.shape
+    half = depth // ways // 2
+    units = hidden.shape[1]
+    return whole_call(
+        ffn_grads_kernel,
+        [((2, ways, half, 2 * units), B16), ((2, ways, units // 2, depth // ways), B16)],
+        [],
+        6 * length * depth * units,
+        "ffn_grads",
+    )(rows, dgu, hidden, out)
+
+
+def cat_grads(ways, width, rows, dproj):
+    length, depth = rows.shape
+    return whole_call(
+        grad_columns,
+        [((2, ways, depth // ways // 2, width), B16)],
+        [],
+        2 * length * depth * width,
+        "cat_grads",
+    )(rows, dproj)[0]
+
+
+def out_grads(ways, lows, back):
+    length, depth = back.shape
+    units = lows.shape[1]
+    return whole_call(
+        grad_rows,
+        [((2, ways, units // 2, depth // ways), B16)],
+        [],
+        2 * length * depth * units,
+        "out_grads",
+    )(lows, back)[0]
+
+
+def exchange_kernel(plan, *refs):
+    refs = list(refs)
+    take = lambda count: [refs.pop(0) for _ in range(count)]
+    part_ref = take(1)[0] if plan.scatter else None
+    local_refs = take(plan.locals)
+    out_refs = take(plan.outs)
+    rows_ref = take(1)[0] if plan.gather else None
+    if plan.scatter:
+        pair_in, far_out, far_in, pair_send, pair_recv, far_send, far_recv = take(7)
+    if plan.gather:
+        give_send, give_recv, spread_send, spread_recv = take(4)
+
+    members, pieces = plan.members, plan.pieces
+    pairs = members // 2
+    me = lax.axis_index("tensor")
+    mine, side = me // 2, me % 2
+    sibling = 2 * mine + 1 - side
+    size = plan.rows // pieces
+
+    def far(k):
+        return 2 * ((mine + k) % pairs) + side
+
+    def across(k):
+        return 2 * ((mine + k) % pairs) + 1 - side
+
+    def rows_of(member, c):
+        return pl.ds(pl.multiple_of(member * plan.rows + c * size, size), size)
+
+    def chunk(c):
+        return pl.ds(c * size, size)
+
+    def copy(source, target, send, receive, member):
+        return pltpu.make_async_remote_copy(
+            src_ref=source, dst_ref=target, send_sem=send, recv_sem=receive,
+            device_id={"tensor": member}, device_id_type=pl.DeviceIdType.MESH,
+        )
+
+    barrier = pltpu.get_barrier_semaphore()
+    for member in [sibling] + [far(k) for k in range(1, pairs)]:
+        pl.semaphore_signal(
+            barrier, inc=1, device_id={"tensor": member}, device_id_type=pl.DeviceIdType.MESH
+        )
+    pl.semaphore_wait(barrier, pairs)
+
+    if plan.scatter:
+        to_pair = {}
+        for c in range(pieces):
+            for k in range(1, pairs):
+                to_pair[k, c] = copy(
+                    part_ref.at[rows_of(across(k), c), :], pair_in.at[k, chunk(c), :],
+                    pair_send.at[k, c], pair_recv.at[k, c], sibling,
+                )
+                to_pair[k, c].start()
+        for c in range(pieces):
+            to_pair[0, c] = copy(
+                part_ref.at[rows_of(sibling, c), :], pair_in.at[0, chunk(c), :],
+                pair_send.at[0, c], pair_recv.at[0, c], sibling,
+            )
+            to_pair[0, c].start()
+        to_far = {}
+        for c in range(pieces):
+            for k in range(1, pairs):
+                to_pair[k, c].wait_recv()
+                far_out[k - 1, chunk(c), :] = (
+                    part_ref[rows_of(far(k), c), :].astype(F32)
+                    + pair_in[k, chunk(c), :].astype(F32)
+                ).astype(B16)
+                to_far[k, c] = copy(
+                    far_out.at[k - 1, chunk(c), :], far_in.at[pairs - k - 1, chunk(c), :],
+                    far_send.at[k - 1, c], far_recv.at[pairs - k - 1, c], far(k),
+                )
+                to_far[k, c].start()
+
+    given, spreads = {}, {}
+    for c in range(pieces):
+        total = None
+        if plan.scatter:
+            to_pair[0, c].wait_recv()
+            total = part_ref[rows_of(me, c), :].astype(F32) + pair_in[0, chunk(c), :].astype(F32)
+            for k in range(1, pairs):
+                copy(
+                    far_out.at[k - 1, chunk(c), :], far_in.at[k - 1, chunk(c), :],
+                    far_send.at[k - 1, c], far_recv.at[k - 1, c], far(k),
+                ).wait_recv()
+                total += far_in[k - 1, chunk(c), :].astype(F32)
+        result = plan.work(c, chunk(c), total, local_refs, out_refs)
+        if plan.gather:
+            own = rows_ref.at[rows_of(me, c), :]
+            rows_ref[rows_of(me, c), :] = result
+            for k in range(1, pairs):
+                spreads[k, c] = copy(
+                    own, own, spread_send.at[k - 1, c], spread_recv.at[pairs - k - 1, c], far(k)
+                )
+                spreads[k, c].start()
+            given[0, c] = copy(own, own, give_send.at[0, c], give_recv.at[0, c], sibling)
+            given[0, c].start()
+    if plan.gather:
+        for c in range(pieces):
+            for k in range(1, pairs):
+                block = rows_ref.at[rows_of(far(k), c), :]
+                copy(
+                    block, block, spread_send.at[k - 1, c], spread_recv.at[k - 1, c], far(k)
+                ).wait_recv()
+                given[k, c] = copy(block, block, give_send.at[k, c], give_recv.at[k, c], sibling)
+                given[k, c].start()
+        for c in range(pieces):
+            for k in range(pairs):
+                block = rows_ref.at[rows_of(sibling if k == 0 else across(k), c), :]
+                copy(block, block, give_send.at[k, c], give_recv.at[k, c], sibling).wait_recv()
+        for c in range(pieces):
+            for k in range(pairs):
+                given[k, c].wait_send()
+            for k in range(1, pairs):
+                spreads[k, c].wait_send()
+    if plan.scatter:
+        for c in range(pieces):
+            for k in range(pairs):
+                to_pair[k, c].wait_send()
+            for k in range(1, pairs):
+                to_far[k, c].wait_send()
+
+
+class Plan:
+    def __init__(self, members, rows, pieces, scatter, gather, count, outs, work):
+        self.members = members
+        self.rows = rows
+        self.pieces = pieces
+        self.scatter = scatter
+        self.gather = gather
+        self.locals = count
+        self.outs = outs
+        self.work = work
+
+
+def exchange(name, number, members, part, local, outs, work, gather, pieces=4):
+    rows, depth = local[0].shape
+    scatter = part is not None
+    pairs = members // 2
+    plan = Plan(members, rows, pieces, scatter, gather, len(local), len(outs), work)
+    vmem = pl.BlockSpec(memory_space=pltpu.VMEM)
+    shapes = [jax.ShapeDtypeStruct(s, t) for s, t in outs]
+    scratch = []
+    dma = pltpu.SemaphoreType.DMA
+    if scatter:
+        wide = part.shape[1]
+        others = max(pairs - 1, 1)
+        scratch += [
+            pltpu.VMEM((pairs, rows, wide), B16),
+            pltpu.VMEM((others, rows, wide), B16),
+            pltpu.VMEM((others, rows, wide), B16),
+            dma((pairs, pieces)), dma((pairs, pieces)), dma((others, pieces)), dma((others, pieces)),
+        ]
+    if gather:
+        shapes.append(jax.ShapeDtypeStruct((members * rows, depth), B16))
+        others = max(pairs - 1, 1)
+        scratch += [
+            dma((pairs, pieces)), dma((pairs, pieces)), dma((others, pieces)), dma((others, pieces)),
+        ]
+    operands = ([part] if scatter else []) + list(local)
+    return pl.pallas_call(
+        functools.partial(exchange_kernel, plan),
+        out_shape=shapes,
+        in_specs=[vmem] * len(operands),
+        out_specs=[vmem] * len(shapes),
+        scratch_shapes=scratch,
+        compiler_params=pltpu.CompilerParams(
+            collective_id=number, has_side_effects=True, vmem_limit_bytes=VMEM_LIMIT
+        ),
+        cost_estimate=pl.CostEstimate(
+            flops=20_000_000_000, bytes_accessed=50_000_000, transcendentals=0
+        ),
+        name=name,
+    )(*operands)
+
+
+def rms(rows, gain):
+    scale = lax.rsqrt(jnp.mean(rows * rows, axis=-1, keepdims=True) + EPS)
+    return rows * scale * gain
+
+
+def rms_back(rows, gain, grad):
+    scale = lax.rsqrt(jnp.mean(rows * rows, axis=-1, keepdims=True) + EPS)
+    scaled = gain * grad
+    mean = jnp.mean(scaled * rows, axis=-1, keepdims=True)
+    into_gain = jnp.sum(grad * rows * scale, axis=0, keepdims=True)
+    return scale * scaled - rows * (scale * scale * scale * mean), into_gain
+
+
+def work_first(c, at, total, local, outs):
+    x, gain = local
+    return rms(x[at, :].astype(F32), gain[0:1, :]).astype(B16)
+
+
+def work_hand(c, at, total, local, outs):
+    return local[0][at, :]
+
+
+def work_mid(c, at, total, local, outs):
+    x, gain = local
+    residual = x[at, :].astype(F32) + total
+    outs[0][at, :] = residual
+    return rms(residual, gain[0:1, :]).astype(B16)
+
+
+def work_turn(c, at, total, local, outs):
+    residual, gain = local
+    out = (residual[at, :] + total).astype(B16)
+    outs[0][at, :] = out
+    return rms(out.astype(F32), gain[0:1, :]).astype(B16)
+
+
+def work_last(c, at, total, local, outs):
+    outs[0][at, :] = (local[0][at, :] + total).astype(B16)
+
+
+def add_gain(c, ref, row):
+    if c == 0:
+        ref[...] = jnp.zeros_like(ref)
+    ref[0:1, :] += row
+
+
+def work_back_ffn(c, at, total, local, outs):
+    residual, cotangent, gain = local
+    step, into_gain = rms_back(residual[at, :], gain[0:1, :], total)
+    grad = cotangent[at, :].astype(F32) + step
+    outs[0][at, :] = grad
+    add_gain(c, outs[1], into_gain)
+    return grad.astype(B16)
+
+
+def work_back_mix(c, at, total, local, outs):
+    x, d_residual, gain = local
+    depth = x.shape[1]
+    step, into_gain = rms_back(x[at, :].astype(F32), gain[0:1, :], total[:, :depth])
+    grad = (d_residual[at, :] + step).astype(B16)
+    outs[0][at, :] = grad
+    outs[2][at, :] = total[:, depth:].astype(B16)
+    add_gain(c, outs[1], into_gain)
+    return grad
+
+
 def widen(block, axis, size):
     missing = size - block.shape[axis]
     if missing == 0:
@@ -526,28 +845,6 @@
     pads = [(0, 0)] * block.ndim
     pads[axis] = (0, missing)
     return jnp.pad(block, pads)
-
-
-def rms(rows, gain):
-    scale = lax.rsqrt(jnp.mean(rows * rows, axis=-1, keepdims=True) + EPS)
-    return rows * scale * gain
-
-
-def rms_back(rows, gain, grad):
-    scale = lax.rsqrt(jnp.mean(rows * rows, axis=-1, keepdims=True) + EPS)
-    scaled = gain * grad
-    mean = jnp.mean(scaled * rows, axis=-1, keepdims=True)
-    return scale * scaled - rows * (scale * scale * scale * mean), jnp.sum(
-        grad * rows * scale, axis=0
-    )
-
-
-def gather_rows(block):
-    return lax.all_gather(block, "tensor", axis=0, tiled=True)
-
-
-def scatter_rows(block):
-    return lax.psum_scatter(block, "tensor", scatter_dimension=0, tiled=True).astype(F32)
 
 
 def on_device(
@@ -601,6 +898,19 @@
     heads_all = lax.all_gather(jnp.concatenate([a_log, dt_bias, d_skip]), "pipe", axis=0)
 
     core_rows = width + LANES
+    wide = cols.total - cols.b
+    source, target = iotas(wide, wide)
+    kind = source // LANES
+    wanted = jnp.where(
+        kind < 2,
+        source,
+        jnp.where(
+            kind < 4,
+            2 * NS + (kind - 2) * KVH * HD + group * HD + source % HD,
+            source + member * heads,
+        ),
+    )
+    fold = ((target == wanted) & (source < 4 * LANES + heads)).astype(B16)
     sub = jnp.arange(width)[:, None] // HD == jnp.arange(LANES)[None, :]
     layers = []
     for layer in range(2):
@@ -613,106 +923,126 @@
                 wout=wout_all[layer, :, :core_rows],
                 wdown=wout_all[layer, :, core_rows : core_rows + units],
                 wgu=gates_all[layer],
-                gains=gains,
+                mix=jnp.broadcast_to(gains[:1], (8, depth)),
+                ffn=jnp.broadcast_to(gains[1:], (8, depth)),
                 hp=hp,
                 dsk=jnp.broadcast_to(jnp.repeat(hp[2, :even], HD)[None], (8, width)),
                 group=sub.astype(B16),
             )
         )
 
-    x = lax.dynamic_index_in_dim(acts_in, section, 0, False).astype(F32)
+    members = lax.axis_size("tensor")
+    rows = acts_in.shape[1]
+    x = lax.dynamic_index_in_dim(acts_in, section, 0, False)
     y_grad = lax.dynamic_index_in_dim(out_grad, section, 0, False)
-    kept = []
-    for w in layers:
-        rows_mix = gather_rows(rms(x, w["gains"][0]).astype(B16))
+    wide = cols.total - cols.b
+    block, block32, gain_row = ((rows, depth), B16), ((rows, depth), F32), ((8, depth), F32)
+
+    def run(name, number, part, local, outs, work, gather):
+        return exchange(name, number, members, part, local, outs, work, gather)
+
+    acts, kept = [], []
+    first, second = layers
+    rows_mix = run("first", 0, None, [x, first["mix"]], [], work_first, True)[0]
+    rows_out = run("hand", 1, None, [y_grad], [], work_hand, True)[0]
+    for layer, w in enumerate(layers):
         *saved, part = core_fwd(cols, rows_mix, w["wcat"], w["wout"], w["hp"], w["dsk"])
-        residual = x + scatter_rows(part)
-        rows_ffn = gather_rows(rms(residual, w["gains"][1]).astype(B16))
+        residual, rows_ffn = run(
+            f"mid_{layer}", 2 + layer, part, [x, w["ffn"]], [block32], work_mid, True
+        )
         gu, hidden, part = ffn_fwd(rows_ffn, w["wgu"], w["wdown"])
-        out = (residual + scatter_rows(part)).astype(B16)
-        kept.append((x, rows_mix, saved, residual, rows_ffn, gu, hidden, out))
-        x = out.astype(F32)
-
-    x_grads, grads = [None, None], [None, None]
+        kept.append((x, rows_mix, saved, residual, rows_ffn, gu, hidden))
+        if layer == 0:
+            x, rows_mix = run(
+                "turn", 4, part, [residual, second["mix"]], [block], work_turn, True
+            )
+            acts.append(x)
+        else:
+            acts += run("last", 5, part, [residual], [block], work_last, False)
+
+    def swap(block):
+        return lax.ppermute(block, "pipe", [(0, 1), (1, 0)])
+
+    def pick(pair):
+        return jnp.where(section == 0, pair[0], pair[1])
+
+    def other(pair):
+        return jnp.where(section == 0, pair[1], pair[0])
+
+    def by_section(mine, received):
+        return jnp.where(section == 0, jnp.stack([mine, received]), jnp.stack([received, mine]))
+
+    def half_sum(halves):
+        received = swap(lax.dynamic_index_in_dim(halves, 1 - section, 0, False))
+        mine = lax.dynamic_index_in_dim(halves, section, 0, False)
+        total = (mine.astype(F32) + received.astype(F32)).astype(B16)
+        return lax.psum_scatter(total, "dp", scatter_dimension=0, tiled=False)
+
+    x_grads, gains, head_grads, sums = [None] * 2, [None] * 2, [None] * 2, [None] * 2
     for layer in (1, 0):
         w = layers[layer]
-        x, rows_mix, saved, residual, rows_ffn, gu, hidden, _ = kept[layer]
-        rows_out = gather_rows(y_grad)
+        x, rows_mix, saved, residual, rows_ffn, gu, hidden = kept[layer]
         dgu, part = ffn_bwd(rows_out, w["wgu"], w["wdown"], gu)
-        step_back, gain_ffn = rms_back(residual, w["gains"][1], scatter_rows(part))
-        d_residual = y_grad.astype(F32) + step_back
-        rows_back = gather_rows(d_residual.astype(B16))
-        dproj, head_grads, part = core_bwd(
-            cols, rows_back, w["wcat"], w["wout"], w["hp"], w["dsk"], w["group"], saved
+        d_residual, gain_ffn, rows_back = run(
+            f"back_ffn_{layer}", 6 + layer, part, [residual, y_grad, w["ffn"]],
+            [block32, gain_row], work_back_ffn, True,
         )
-        step_back, gain_mix = rms_back(x, w["gains"][0], scatter_rows(part))
-        y_grad = (d_residual + step_back).astype(B16)
+        g_gu, g_down = ffn_grads(dp, rows_ffn, dgu, hidden, rows_out)
+        g_out = out_grads(dp, saved[3], rows_back)
+        dproj, head_grads[layer], part = core_bwd(
+            cols, members, rows_back, w["wcat"], w["wout"], w["hp"], w["dsk"], w["group"],
+            rows_mix, fold, saved,
+        )
+        y_grad, gain_mix, shared_part, *more = run(
+            f"back_mix_{layer}", 8 + layer, part, [x, d_residual, w["mix"]],
+            [block, gain_row, ((rows, wide), B16)], work_back_mix, layer == 1,
+        )
+        rows_out = more[0] if more else None
         x_grads[layer] = y_grad
-        g_gu = tn(rows_ffn, dgu).astype(B16)
-        g_cat = tn(rows_mix, dproj).astype(B16)
-        lows = saved[3]
-        by_piece = lambda rows: rows.reshape(rows.shape[0], dp, piece)
-        g_down = jnp.einsum("lf,lkd->kfd", hidden, by_piece(rows_out), preferred_element_type=F32)
-        g_out = jnp.einsum("lf,lkd->kfd", lows, by_piece(rows_back), preferred_element_type=F32)
-        g_rows = jnp.concatenate([g_out, g_down], axis=1).astype(B16)
-        g_cols = jnp.concatenate([g_cat[:, : cols.b], g_gu], axis=1)
-        g_kv = g_cat[:, cols.k : cols.k + 2 * LANES].astype(F32).reshape(depth, 2, 2, HD).sum(2)
-        g_kv = lax.dynamic_update_slice(
-            jnp.zeros((depth, 2, KVH, HD), F32), g_kv[:, :, None, :], (0, 0, group, 0)
+        g_cat = cat_grads(dp, cols.b, rows_mix, dproj)
+        gains[layer] = jnp.stack([gain_mix[0], gain_ffn[0]])
+        shared_sum = lax.psum_scatter(
+            shared_part.reshape(dp, rows // dp, wide), "dp", scatter_dimension=0, tiled=False
         )
-        g_step = lax.dynamic_update_slice_in_dim(
-            jnp.zeros((depth, LANES), F32),
-            g_cat[:, cols.step : cols.step + heads].astype(F32), member * heads, 1,
-        )
-        g_shared = jnp.concatenate(
-            [g_cat[:, cols.b : cols.k].astype(F32), g_kv.reshape(depth, -1), g_step], axis=1
-        ).astype(B16)
-        small = jnp.concatenate([gain_mix, gain_ffn])
-        grads[layer] = (
-            lax.psum_scatter(g_cols, "dp", scatter_dimension=0, tiled=True),
-            lax.psum_scatter(g_rows, "dp", scatter_dimension=0, tiled=False),
-            lax.psum_scatter(g_shared, ("dp", "tensor"), scatter_dimension=0, tiled=True),
-            small,
-            head_grads[:3, :heads],
-        )
-
-    def swap(own, other):
-        return lax.ppermute(jnp.where(section == 0, other, own), "pipe", [(0, 1), (1, 0)])
-
-    def pick(pair):
-        return jnp.where(section == 0, pair[0], pair[1])
-
-    def placed(pair):
-        mine, received = pick(pair), swap(*pair)
-        return jnp.where(
-            section == 0, jnp.stack([mine, received]), jnp.stack([received, mine])
-        )
-
-    acts = placed([k[-1] for k in kept])
-    in_grads = placed(x_grads)
-    totals = [
-        pick(pair).astype(F32) + swap(*pair).astype(F32)
-        for pair in zip(grads[0][:3], grads[1][:3])
+        sums[layer] = [half_sum(g) for g in (g_gu, g_down, g_out, g_cat)] + [shared_sum]
+
+    acts = by_section(pick(acts), swap(other(acts)))
+    in_grads = by_section(pick(x_grads), swap(other(x_grads)))
+    pairs = list(zip(*sums))
+    g_gates, g_down, g_out, g_cat = [
+        by_section(pick(pair), swap(other(pair))).reshape((-1,) + pair[0].shape[1:]).astype(F32)
+        for pair in pairs[:4]
     ]
-    small = jnp.stack([g[3] for g in grads]).reshape(2, 2, depth)
-    small = lax.psum(lax.psum_scatter(small, ("dp", "tensor"), scatter_dimension=2, tiled=True), "pipe")
-    head_sum = lax.psum(jnp.stack([g[4] for g in grads]), both)
-    g_cols, g_rows, g_shared = totals
-    g_mixer = jnp.stack([g_cols[:, :real], g_cols[:, width : width + real]], axis=1)
-    g_gates = g_cols[:, cols.b :].reshape(piece, 2, units)
+    g_shared = pick(pairs[4]).astype(F32) + swap(other(pairs[4])).astype(F32)
+    slots = [
+        lax.dynamic_update_index_in_dim(
+            jnp.zeros((members, 3, heads), F32), h[:3, :heads], member, 0
+        ).reshape(-1)
+        for h in head_grads
+    ]
+    small = jnp.stack([jnp.concatenate([g.reshape(-1), s]) for g, s in zip(gains, slots)])
+    small = lax.psum(small, ("pipe", "dp", "tensor"))
+    small = lax.dynamic_index_in_dim(small, section, 0, False)
+    place = lax.axis_index("dp") * members + member
+    share = depth // (dp * members)
+    g_gains = lax.dynamic_slice_in_dim(small[: 2 * depth].reshape(2, depth), place * share, share, 1)
+    g_heads = small[2 * depth :].reshape(members, 3, heads)
+    g_heads = lax.dynamic_index_in_dim(g_heads, member, 0, False)
+    g_mixer = jnp.stack([g_cat[:, :real], g_cat[:, width : width + real]], axis=1)
+    table = 2 * NS + 2 * KVH * HD
     return (
         acts[None],
         in_grads[None],
-        pick(small)[None],
+        g_gains[None],
         g_mixer[None],
-        g_cols[None, :, cols.q : cols.q + q_real],
-        g_shared[None, :, : 2 * NS + 2 * KVH * HD],
-        g_shared[None, :, 2 * NS + 2 * KVH * HD :][:, :, :HM],
-        pick(head_sum)[None],
-        g_rows[None, :real],
-        g_rows[None, width : width + q_real],
-        g_gates[None],
-        g_rows[None, core_rows:],
+        g_cat[None, :, cols.q : cols.q + q_real],
+        g_shared[None, :, :table],
+        g_shared[None, :, table : table + HM],
+        g_heads[None],
+        g_out[None, :real],
+        g_out[None, width : width + q_real],
+        g_gates.reshape(1, piece, 2, units),
+        g_down[None],
     )
 
 

time: 1320 us -> 970 us (0.73)
  waiting for transfers between devices: 932 us -> 328 us
  Pallas kernels: 140 us -> 464 us
  matrix products: 39 us -> 0 us
  local copies, waits for them, and re-layouts: 83.3 us -> 49.1 us
  other arithmetic: 65.7 us -> 35.9 us
  blocking collectives: 27 us -> 47.3 us
    reduce_scatter x14 -> x10, waiting for transfers between devices: 445 us -> 7.39 us  [the longest x8 7.38 us: half_sum(): return lax.psum_scatter(total, 'dp', scatter_dimension=0, tiled=False)]
    pallas_call x0 -> x10, Pallas kernels: none -> 277 us  [exchange(): pl.pallas_call(functools.partial(exchange_kernel, plan), out_shape=shapes...]
    all_gather x8 -> x0, waiting for transfers between devices: 163 us -> none  [gather_rows(): return lax.all_gather(block, 'tensor', axis=0, tiled=True)]
    ppermute x5 -> x15, waiting for transfers between devices: 32.6 us -> 133 us  [swap(): return lax.ppermute(block, 'pipe', [(0, 1), (1, 0)])]
    unnamed x27 -> x13, waiting for transfers between devices: 59.6 us -> 0.21 us
    pallas_call x8 -> x14, Pallas kernels: 140 us -> 187 us  [call(): pl.pallas_call(kernel, out_shape=[jax.ShapeDtypeStruct(s, t) for s, t in...]
    dot_general x8 -> x0, matrix products: 39 us -> none  [the longest x4 24.4 us: tn(): lax.dot_general(a, b, (((0,), (0,)), ((), ())), preferred_element_type=F32)]
    all_gather x1, waiting for transfers between devices: 71.5 us -> 41.5 us  [on_device(): lax.all_gather(gates, both, axis=0, tiled=True).reshape(2, depth, 2 * units)]
  transfers between devices with their start and end apart: 31 -> 28, of which waited for: 26 -> 17; matrix products, arithmetic and copies ran while one was open for 12% -> 7% of each run, Pallas kernels for 1% -> 9%
where the time goes in v1:
time: 970 us; the launch traced here: 956 us
  Pallas kernels  464 us (48%)
  waiting for transfers between devices  328 us (34%)
  local copies, waits for them, and re-layouts  49.1 us (5%)
  blocking collectives  47.3 us (5%)
  other arithmetic  35.9 us (4%)
  starting transfers between devices  16.3 us (2%)
  between operations  14.9 us (2%)
    pallas_call x10, Pallas kernels, exchange(): pl.pallas_call(functools.partial(exchange_kernel, plan), out_shape=shapes...  277 us
    pallas_call x14, Pallas kernels, call(): pl.pallas_call(kernel, out_shape=[jax.ShapeDtypeStruct(s, t) for s, t in...  187 us
    ppermute x15, waiting for transfers between devices, swap(): return lax.ppermute(block, 'pipe', [(0, 1), (1, 0)])  133 us
    all_gather x1, waiting for transfers between devices, on_device(): lax.all_gather(wcat, both, axis=0, tiled=True).reshape(2, depth, cols.total)  75.8 us
    all_gather x1, waiting for transfers between devices, on_device(): wout_all = lax.all_gather(wout, both, axis=0)  70.5 us
    psum x1, blocking collectives, on_device(): small = lax.psum(small, ('pipe', 'dp', 'tensor'))  42.9 us
    all_gather x1, waiting for transfers between devices, on_device(): lax.all_gather(gates, both, axis=0, tiled=True).reshape(2, depth, 2 * units)  41.5 us
  transfers between devices with their start and end apart: 28, of which 17 were waited for; matrix products, arithmetic and copies ran while one was open for 7% of the time, Pallas kernels for 9%

profile of v1, /device:TPU:8, one launch (start us, length us, event | category | flops | bytes accessed | tf_op | source)
XLA Modules:
  0.0 955.9 jit_solution(14556004115980850280)
XLA Ops:
  25.5 17.7 %hand.1.out_ref = bf16[1024,1024]{1,0:T(8,128)(2,1)} custom-call(bf16[256,1024]{1,0:T(8,128)(2,1)} %dynamic-slice_bitcast_fusion.8.refs_0_.refs_2_), custom_call_target="tpu_custom_call" | custom-call | flops 20000000000 | bytes 50000000 | tf_op jit(solution)/shard_map/hand/pallas_call | solution.py:759
  43.2 41.5 %all-gather.9.cloned.1.call-done = bf16[2048,1024]{1,0:T(8,128)(2,1)} async-done(((bf16[256,1024]{1,0:T(8,128)(2,1)}), bf16[2048,1024]{1,0:T(8,128)(2,1)}) %all-gather.9.cloned.1.call-update) | async-done | bytes 4194320 | tf_op jit(solution)/shard_map/all_gather | solution.py:896
  89.3 70.5 %all-gather.11.cloned.1.call-done = bf16[8320,256]{1,0:T(8,128)(2,1)} async-done(((bf16[1040,256]{1,0:T(8,128)(2,1)}), bf16[8320,256]{1,0:T(8,128)(2,1)}) %all-gather.11.cloned.1.call-update) | async-done | bytes 4259856 | tf_op jit(solution)/shard_map/all_gather | solution.py:895
  165.5 17.8 %first.1.rows_ref = bf16[1024,1024]{1,0:T(8,128)(2,1)} custom-call(bf16[256,1024]{1,0:T(8,128)(2,1)} %dynamic-slice_bitcast_fusion.9.refs_0_.refs_1_, f32[8,1024]{1,0:T(8,128)} %broadcast_in_dim.83.refs_1_.refs_3_), custom_call_target="tpu_custom_call" | custom-call | flops 20000000000 | bytes 50000000 | tf_op jit(solution)/shard_map/first/pallas_call | solution.py:759
  183.3 75.8 %all-gather.7.cloned.1.call-done = bf16[2048,1536]{1,0:T(8,128)(2,1)} async-done(((bf16[256,1536]{1,0:T(8,128)(2,1)}), bf16[2048,1536]{1,0:T(8,128)(2,1)}) %all-gather.7.cloned.1.call-update) | async-done | bytes 6291472 | tf_op jit(solution)/shard_map/all_gather | solution.py:894
  265.6 22.2 %core_fwd.2 = (bf16[1024,1408]{1,0:T(8,128)(2,1)}, f32[1024,128]{1,0:T(8,128)}, bf16[1024,384]{1,0:T(8,128)(2,1)}, bf16[1024,512]{1,0:T(8,128)(2,1)}, bf16[8,128...) custom-call(bf16[1024,1024]{1,0:T(8,128)(2,1)} %first.1.rows_ref, ...), custom_call_target="tpu_custom_call" | custom-call | flops 32212254720 | bytes 12615680 | tf_op jit(solution)/shard_map/core_fwd/pallas_call | solution.py:462
  288.3 31.6 %mid_0.1 = (f32[256,1024]{1,0:T(8,128)}, bf16[1024,1024]{1,0:T(8,128)(2,1)}) custom-call(bf16[1024,1024]{1,0:T(8,128)(2,1)} %get-tuple-element.65.refs_0_, bf16[256,1024]{1,0:T(8,128)(2,1)} %dynamic-slice_bitcast_fusion.9.refs_0_.refs_1_, f32[8,1024]{1,0:T(8,128)} %broadcast_in_dim.88.refs_2_.refs_3_), custom_call_target="tpu_custom_call" | custom-call | flops 20000000000 | bytes 50000000 | tf_op jit(solution)/shard_map/mid_0/pallas_call | solution.py:759
  320.0 9.1 ffn_fwd.2
  329.7 31.7 %turn.1 = (bf16[256,1024]{1,0:T(8,128)(2,1)}, bf16[1024,1024]{1,0:T(8,128)(2,1)}) custom-call(bf16[1024,1024]{1,0:T(8,128)(2,1)} %get-tuple-element.67.refs_0_, f32[256,1024]{1,0:T(8,128)} %get-tuple-element.68.refs_1_, f32[8,1024]{1,0:T(8,128)} %broadcast_in_dim.90.refs_2_.refs_3_), custom_call_target="tpu_custom_call" | custom-call | flops 20000000000 | bytes 50000000 | tf_op jit(solution)/shard_map/turn/pallas_call | solution.py:759
  362.0 22.1 %core_fwd.3 = (bf16[1024,1408]{1,0:T(8,128)(2,1)}, f32[1024,128]{1,0:T(8,128)}, bf16[1024,384]{1,0:T(8,128)(2,1)}, bf16[1024,512]{1,0:T(8,128)(2,1)}, bf16[8,128...) custom-call(bf16[1024,1024]{1,0:T(8,128)(2,1)} %get-tuple-element.70.rows_ref, ...), custom_call_target="tpu_custom_call" | custom-call | flops 32212254720 | bytes 12615680 | tf_op jit(solution)/shard_map/core_fwd/pallas_call | solution.py:462
  384.7 31.6 %mid_1.1 = (f32[256,1024]{1,0:T(8,128)}, bf16[1024,1024]{1,0:T(8,128)(2,1)}) custom-call(bf16[1024,1024]{1,0:T(8,128)(2,1)} %get-tuple-element.71.refs_0_, bf16[256,1024]{1,0:T(8,128)(2,1)} %get-tuple-element.69.refs_1_, f32[8,1024]{1,0:T(8,128)} %broadcast_in_dim.95.refs_2_.refs_3_), custom_call_target="tpu_custom_call" | custom-call | flops 20000000000 | bytes 50000000 | tf_op jit(solution)/shard_map/mid_1/pallas_call | solution.py:759
  416.4 9.0 ffn_fwd.3
  425.4 10.2 %ffn_bwd.2 = (bf16[1024,1024]{1,0:T(8,128)(2,1)}, bf16[1024,1024]{1,0:T(8,128)(2,1)}) custom-call(bf16[1024,1024]{1,0:T(8,128)(2,1)} %hand.1.out_ref, bf16[1024,1024]{1,0:T(8,128)(2,1)} %get-tuple-element.162.wgu_ref, bf16[4,512,256]{2,1,0:T(8,128)(2,1)} %get-tuple-element.156.wdown_ref, bf16[1024,1024]{1,0:T(8,128)(2,1)} %get-tuple-element.75.gu_ref), custom_call_target="tpu_custom_call" | custom-call | flops 3221225472 | bytes 14680064 | tf_op jit(solution)/shard_map/ffn_bwd/pallas_call | solution.py:462
  435.6 31.8 %back_ffn_1.1 = (f32[256,1024]{1,0:T(8,128)}, f32[8,1024]{1,0:T(8,128)}, bf16[1024,1024]{1,0:T(8,128)(2,1)}) custom-call(bf16[1024,1024]{1,0:T(8,128)(2,1)} %get-tuple-element.76.refs_0_, f32[256,1024]{1,0:T(8,128)} %get-tuple-element.74.refs_1_, bf16[256,1024]{1,0:T(8,128)(2,1)} %dynamic-slice_bitcast_fusion.8.refs_0_.refs_2_, ...), custom_call_target="tpu_custom_call" | custom-call | flops 20000000000 | bytes 50000000 | tf_op jit(solution)/shard_map/back_ffn_1/pallas_call | solution.py:759
  467.5 33.9 %core_bwd.2 = (bf16[1024,1536]{1,0:T(8,128)(2,1)}, f32[8,128]{1,0:T(8,128)}, bf16[1024,1664]{1,0:T(8,128)(2,1)}) custom-call(bf16[1024,1024]{1,0:T(8,128)(2,1)} %get-tuple-element.77.back_ref, bf16[1024,1536]{1,0:T(8,128)(2,1)} %get-tuple-element.154.wcat_ref, bf16[4,512,256]{2,1,0:T(8,128)(2,1)} %get-tuple-element.157.wout_ref, f32[8,128]{1,0:T(8,128)} %pad.76.hp_ref, ...), custom_call_target="tpu_custom_call" | custom-call | flops 64424509440 | bytes 30834688 | tf_op jit(solution)/shard_map/core_bwd/pallas_call | solution.py:462
  501.3 39.4 %back_mix_1.1 = (bf16[256,1024]{1,0:T(8,128)(2,1)}, f32[8,1024]{1,0:T(8,128)}, bf16[256,640]{1,0:T(8,128)(2,1)}, bf16[1024,1024]{1,0:T(8,128)(2,1)}) custom-call(bf16[1024,1664]{1,0:T(8,128)(2,1)} %get-tuple-element.84.refs_0_, bf16[256,1024]{1,0:T(8,128)(2,1)} %get-tuple-element.69.refs_1_, f32[256,1024]{1,0:T(8,128)} %get-tuple-element.85.refs_2_, ...), custom_call_target="tpu_custom_call" | custom-call | flops 20000000000 | bytes 50000000 | tf_op jit(solution)/shard_map/back_mix_1/pallas_call | solution.py:759
  540.7 9.9 %ffn_bwd.3 = (bf16[1024,1024]{1,0:T(8,128)(2,1)}, bf16[1024,1024]{1,0:T(8,128)(2,1)}) custom-call(bf16[1024,1024]{1,0:T(8,128)(2,1)} %get-tuple-element.86.out_ref, bf16[1024,1024]{1,0:T(8,128)(2,1)} %get-tuple-element.163.wgu_ref, bf16[4,512,256]{2,1,0:T(8,128)(2,1)} %get-tuple-element.158.wdown_ref, bf16[1024,1024]{1,0:T(8,128)(2,1)} %get-tuple-element.87.gu_ref), custom_call_target="tpu_custom_call" | custom-call | flops 3221225472 | bytes 14680064 | tf_op jit(solution)/shard_map/ffn_bwd/pallas_call | solution.py:462
  550.6 31.8 %back_ffn_0.1 = (f32[256,1024]{1,0:T(8,128)}, f32[8,1024]{1,0:T(8,128)}, bf16[1024,1024]{1,0:T(8,128)(2,1)}) custom-call(bf16[1024,1024]{1,0:T(8,128)(2,1)} %get-tuple-element.88.refs_0_, f32[256,1024]{1,0:T(8,128)} %get-tuple-element.68.refs_1_, bf16[256,1024]{1,0:T(8,128)(2,1)} %get-tuple-element.89.refs_2_, f32[8,1024]{1,0:T(8,128)} %broadcast_in_dim.88.refs_2_.refs_3_), custom_call_target="tpu_custom_call" | custom-call | flops 20000000000 | bytes 50000000 | tf_op jit(solution)/shard_map/back_ffn_0/pallas_call | solution.py:759
  582.5 34.1 %core_bwd.3 = (bf16[1024,1536]{1,0:T(8,128)(2,1)}, f32[8,128]{1,0:T(8,128)}, bf16[1024,1664]{1,0:T(8,128)(2,1)}) custom-call(bf16[1024,1024]{1,0:T(8,128)(2,1)} %get-tuple-element.90.back_ref, bf16[1024,1536]{1,0:T(8,128)(2,1)} %get-tuple-element.155.wcat_ref, bf16[4,512,256]{2,1,0:T(8,128)(2,1)} %get-tuple-element.159.wout_ref, f32[8,128]{1,0:T(8,128)} %pad.75.hp_ref, ...), custom_call_target="tpu_custom_call" | custom-call | flops 64424509440 | bytes 30834688 | tf_op jit(solution)/shard_map/core_bwd/pallas_call | solution.py:462
  616.5 26.4 %back_mix_0.1 = (bf16[256,1024]{1,0:T(8,128)(2,1)}, f32[8,1024]{1,0:T(8,128)}, bf16[256,640]{1,0:T(8,128)(2,1)}) custom-call(bf16[1024,1664]{1,0:T(8,128)(2,1)} %get-tuple-element.97.refs_0_, bf16[256,1024]{1,0:T(8,128)(2,1)} %dynamic-slice_bitcast_fusion.9.refs_0_.refs_1_, f32[256,1024]{1,0:T(8,128)} %get-tuple-element.98.refs_2_, ...), custom_call_target="tpu_custom_call" | custom-call | flops 20000000000 | bytes 50000000 | tf_op jit(solution)/shard_map/back_mix_0/pallas_call | solution.py:759
  649.0 13.1 %collective-permute-done.7 = bf16[4,256,256]{2,1,0:T(8,128)(2,1)S(1)} collective-permute-done((bf16[4,256,256]{2,1,0:T(8,128)(2,1)S(1)}, bf16[4,256,256]{2,1,0:T(8,128)(2,1)S(1)}, u32[]{:S(2)}, u32[]{:S(2)}) %collective-permute-start.7) | collective-permute-done | bytes 524320 | tf_op jit(solution)/shard_map/ppermute | solution.py:964
  670.0 12.3 %collective-permute-done.6 = bf16[4,256,256]{2,1,0:T(8,128)(2,1)S(1)} collective-permute-done((bf16[4,256,256]{2,1,0:T(8,128)(2,1)S(1)}, bf16[4,256,256]{2,1,0:T(8,128)(2,1)S(1)}, u32[]{:S(2)}, u32[]{:S(2)}) %collective-permute-start.6) | collective-permute-done | bytes 524320 | tf_op jit(solution)/shard_map/ppermute | solution.py:964
  684.3 7.6 ffn_grads.3
  693.6 11.3 %collective-permute-done.13 = bf16[4,256,256]{2,1,0:T(8,128)(2,1)S(1)} collective-permute-done((bf16[4,256,256]{2,1,0:T(8,128)(2,1)S(1)}, bf16[4,256,256]{2,1,0:T(8,128)(2,1)S(1)}, u32[]{:S(2)}, u32[]{:S(2)}) %collective-permute-start.13) | collective-permute-done | bytes 524320 | tf_op jit(solution)/shard_map/ppermute | solution.py:964
  707.2 7.6 ffn_grads.2
  729.7 17.0 %collective-permute-done.3 = bf16[4,128,896]{2,1,0:T(8,128)(2,1)} collective-permute-done((bf16[4,128,896]{2,1,0:T(8,128)(2,1)}, bf16[4,128,896]{2,1,0:T(8,128)(2,1)}, u32[]{:S(2)}, u32[]{:S(2)}) %collective-permute-start.3) | collective-permute-done | bytes 917536 | tf_op jit(solution)/shard_map/ppermute | solution.py:964
  758.4 19.6 %collective-permute-done.2 = bf16[4,128,896]{2,1,0:T(8,128)(2,1)S(1)} collective-permute-done((bf16[4,128,896]{2,1,0:T(8,128)(2,1)}, bf16[4,128,896]{2,1,0:T(8,128)(2,1)S(1)}, u32[]{:S(2)}, u32[]{:S(2)}) %collective-permute-start.2) | collective-permute-done | bytes 917536 | tf_op jit(solution)/shard_map/ppermute | solution.py:964
  779.3 17.4 %last.1 = bf16[256,1024]{1,0:T(8,128)(2,1)} custom-call(bf16[1024,1024]{1,0:T(8,128)(2,1)} %get-tuple-element.73.refs_0_, f32[256,1024]{1,0:T(8,128)} %get-tuple-element.74.refs_1_), custom_call_target="tpu_custom_call" | custom-call | flops 20000000000 | bytes 50000000 | tf_op jit(solution)/shard_map/last/pallas_call | solution.py:759
  804.1 20.0 %collective-permute-done.10 = bf16[4,128,1024]{2,1,0:T(8,128)(2,1)} collective-permute-done((bf16[4,128,1024]{2,1,0:T(8,128)(2,1)}, bf16[4,128,1024]{2,1,0:T(8,128)(2,1)}, u32[]{:S(2)}, u32[]{:S(2)}) %collective-permute-start.10) | collective-permute-done | bytes 1048608 | tf_op jit(solution)/shard_map/ppermute | solution.py:964
  826.9 42.9 %psum.7 = f32[2,2120]{1,0:T(2,128)S(1)} all-reduce(f32[2,2120]{1,0:T(2,128)S(1)} %pad_maximum_fusion.1), channel_id=1, replica_groups=mesh['pipe'=2,'dp'=4,'tensor'=4] {'pipe','dp','tensor'}, use_global_device_ids=true, to_apply=%region_0.1 | all-reduce | flops 4240 | bytes 33920 | tf_op jit(solution)/shard_map/psum | solution.py:1024
  889.8 19.5 %collective-permute-done.5 = bf16[64,640]{1,0:T(8,128)(2,1)S(1)} collective-permute-done((bf16[64,640]{1,0:T(8,128)(2,1)S(1)}, bf16[64,640]{1,0:T(8,128)(2,1)S(1)}, u32[]{:S(2)}, u32[]{:S(2)}) %collective-permute-start.5) | collective-permute-done | bytes 81952 | tf_op jit(solution)/shard_map/ppermute | solution.py:964
  930.4 7.3 reduce-scatter.23.cloned.1.call-done
  (213 shorter events, 147.1 us)
Async XLA Ops:
  7.2 77.5 %all-gather.9.cloned.1.call-start = ((), (), s32[]{:S(2)}) async-start(), calls=%async_computation.11 | async-start | bytes 4718592 | tf_op jit(solution)/shard_map/all_gather | solution.py:896
  9.3 150.5 %all-gather.11.cloned.1.call-start = ((), (), s32[]{:S(2)}) async-start(), calls=%async_computation.22 | async-start | bytes 4792320 | tf_op jit(solution)/shard_map/all_gather | solution.py:895
  12.0 247.1 %all-gather.7.cloned.1.call-start = ((), (), s32[]{:S(2)}) async-start(), calls=%async_computation.10 | async-start | bytes 7077888 | tf_op jit(solution)/shard_map/all_gather | solution.py:894
  14.9 864.1 %reduce-scatter.15.cloned.1.call-start = ((), (), s32[]{:S(2)}) async-start(), calls=%async_computation.14 | async-start | bytes 409600 | tf_op jit(solution)/shard_map/reduce_scatter | solution.py:1004
  643.0 236.0 %reduce-scatter.17.cloned.1.call-start = ((), (), s32[]{:S(2)}) async-start(), calls=%async_computation.15 | async-start | bytes 409600 | tf_op jit(solution)/shard_map/reduce_scatter | solution.py:1004
  648.3 13.8 %collective-permute-start.7 = (bf16[4,256,256]{2,1,0:T(8,128)(2,1)S(1)}, bf16[4,256,256]{2,1,0:T(8,128)(2,1)S(1)}, u32[]{:S(2)}, u32[]{:S(2)}) collective-permute-start(bf16[4,256,256]{2,1,0:T(8,128)(2,1)S(1)} %dynamic-slice_bitcast_fusion.6), channel_id=1, source_target_pairs={{0,16},{16,0},{1,17},{17,1},{2,18},{18,2},{3,19},{19,3},{4,20},{20... | collective-permute-start | bytes 1572872 | tf_op jit(solution)/shard_map/ppermute | solution.py:964
  648.9 263.8 %reduce-scatter.21.cloned.1.call-start = ((), (), s32[]{:S(2)}) async-start(), calls=%async_computation.17 | async-start | bytes 655360 | tf_op jit(solution)/shard_map/reduce_scatter | solution.py:979
  664.1 248.7 %reduce-scatter.19.cloned.1.call-start = ((), (), s32[]{:S(2)}) async-start(), calls=%async_computation.16 | async-start | bytes 655360 | tf_op jit(solution)/shard_map/reduce_scatter | solution.py:979
  669.4 12.9 %collective-permute-start.6 = (bf16[4,256,256]{2,1,0:T(8,128)(2,1)S(1)}, bf16[4,256,256]{2,1,0:T(8,128)(2,1)S(1)}, u32[]{:S(2)}, u32[]{:S(2)}) collective-permute-start(bf16[4,256,256]{2,1,0:T(8,128)(2,1)S(1)} %dynamic-slice_bitcast_fusion.7), channel_id=1, source_target_pairs={{0,16},{16,0},{1,17},{17,1},{2,18},{18,2},{3,19},{19,3},{4,20},{20... | collective-permute-start | bytes 1572872 | tf_op jit(solution)/shard_map/ppermute | solution.py:964
  684.2 231.0 %reduce-scatter.29.cloned.1.call-start = ((), (), s32[]{:S(2)}) async-start(), calls=%async_computation.21 | async-start | bytes 655360 | tf_op jit(solution)/shard_map/reduce_scatter | solution.py:979
  693.0 12.0 %collective-permute-start.13 = (bf16[4,256,256]{2,1,0:T(8,128)(2,1)S(1)}, bf16[4,256,256]{2,1,0:T(8,128)(2,1)S(1)}, u32[]{:S(2)}, u32[]{:S(2)}) collective-permute-start(bf16[4,256,256]{2,1,0:T(8,128)(2,1)S(1)} %dynamic-slice_bitcast_fusion.4), channel_id=1, source_target_pairs={{0,16},{16,0},{1,17},{17,1},{2,18},{18,2},{3,19},{19,3},{4,20},{20... | collective-permute-start | bytes 1572872 | tf_op jit(solution)/shard_map/ppermute | solution.py:964
  706.9 208.3 %reduce-scatter.27.cloned.1.call-start = ((), (), s32[]{:S(2)}) async-start(), calls=%async_computation.20 | async-start | bytes 655360 | tf_op jit(solution)/shard_map/reduce_scatter | solution.py:979
  715.9 12.8 %collective-permute-start.12 = (bf16[4,256,256]{2,1,0:T(8,128)(2,1)S(1)}, bf16[4,256,256]{2,1,0:T(8,128)(2,1)S(1)}, u32[]{:S(2)}, u32[]{:S(2)}) collective-permute-start(bf16[4,256,256]{2,1,0:T(8,128)(2,1)S(1)} %dynamic-slice_bitcast_fusion.5), channel_id=1, source_target_pairs={{0,16},{16,0},{1,17},{17,1},{2,18},{18,2},{3,19},{19,3},{4,20},{20... | collective-permute-start | bytes 1572872 | tf_op jit(solution)/shard_map/ppermute | solution.py:964
  722.9 23.8 %copy-start.3 = (bf16[2,4,128,896]{3,2,1,0:T(8,128)(2,1)S(1)}, bf16[2,4,128,896]{3,2,1,0:T(8,128)(2,1)}, u32[]{:S(2)}) copy-start(bf16[2,4,128,896]{3,2,1,0:T(8,128)(2,1)} %cat_grads.3) | copy-start | bytes 5505028
  725.3 21.4 %collective-permute-start.3 = (bf16[4,128,896]{2,1,0:T(8,128)(2,1)}, bf16[4,128,896]{2,1,0:T(8,128)(2,1)}, u32[]{:S(2)}, u32[]{:S(2)}) collective-permute-start(bf16[4,128,896]{2,1,0:T(8,128)(2,1)} %dynamic-slice_bitcast_fusion.2), channel_id=1, source_target_pairs={{0,16},{16,0},{1,17},{17,1},{2,18},{18,2},{3,19},{19,3},{4,20},{20... | collective-permute-start | bytes 2752520 | tf_op jit(solution)/shard_map/ppermute | solution.py:964
  729.6 193.3 %reduce-scatter.13.cloned.1.call-start = ((), (), s32[]{:S(2)}) async-start(), calls=%async_computation.13 | async-start | bytes 1146880 | tf_op jit(solution)/shard_map/reduce_scatter | solution.py:979
  749.1 173.9 %reduce-scatter.11.cloned.1.call-start = ((), (), s32[]{:S(2)}) async-start(), calls=%async_computation.12 | async-start | bytes 1146880 | tf_op jit(solution)/shard_map/reduce_scatter | solution.py:979
  757.7 20.4 %collective-permute-start.2 = (bf16[4,128,896]{2,1,0:T(8,128)(2,1)}, bf16[4,128,896]{2,1,0:T(8,128)(2,1)S(1)}, u32[]{:S(2)}, u32[]{:S(2)}) collective-permute-start(bf16[4,128,896]{2,1,0:T(8,128)(2,1)} %dynamic-slice_bitcast_fusion.3), channel_id=1, source_target_pairs={{0,16},{16,0},{1,17},{17,1},{2,18},{18,2},{3,19},{19,3},{4,20},{20... | collective-permute-start | bytes 2752520 | tf_op jit(solution)/shard_map/ppermute | solution.py:964
  779.2 151.2 %reduce-scatter.25.cloned.1.call-start = ((), (), s32[]{:S(2)}) async-start(), calls=%async_computation.19 | async-start | bytes 1310720 | tf_op jit(solution)/shard_map/reduce_scatter | solution.py:979
  797.8 26.3 %collective-permute-start.10 = (bf16[4,128,1024]{2,1,0:T(8,128)(2,1)}, bf16[4,128,1024]{2,1,0:T(8,128)(2,1)}, u32[]{:S(2)}, u32[]{:S(2)}) collective-permute-start(bf16[4,128,1024]{2,1,0:T(8,128)(2,1)} %dynamic-slice_bitcast_fusion), channel_id=1, source_target_pairs={{0,16},{16,0},{1,17},{17,1},{2,18},{18,2},{3,19},{19,3},{4,20},{20... | collective-permute-start | bytes 3145736 | tf_op jit(solution)/shard_map/ppermute | solution.py:964
  799.2 77.4 %collective-permute-start = (bf16[256,1024]{1,0:T(8,128)(2,1)}, bf16[256,1024]{1,0:T(8,128)(2,1)}, u32[]{:S(2)}, u32[]{:S(2)}) collective-permute-start(bf16[256,1024]{1,0:T(8,128)(2,1)} %get-tuple-element.167), channel_id=1, source_target_pairs={{0,16},{16,0},{1,17},{17,1},{2,18},{18,2},{3,19},{19,3},{4,20},{20... | collective-permute-start | bytes 1572872 | tf_op jit(solution)/shard_map/ppermute | solution.py:964
  826.8 47.6 %copy-start.4 = (bf16[2,4,128,1024]{3,2,1,0:T(8,128)(2,1)S(1)}, bf16[2,4,128,1024]{3,2,1,0:T(8,128)(2,1)}, u32[]{:S(2)}) copy-start(bf16[2,4,128,1024]{3,2,1,0:T(8,128)(2,1)} %get-tuple-element.112) | copy-start | bytes 6291460
  826.8 110.9 %reduce-scatter.23.cloned.1.call-start = ((), (), s32[]{:S(2)}) async-start(), calls=%async_computation.18 | async-start | bytes 1310720 | tf_op jit(solution)/shard_map/reduce_scatter | solution.py:979
  872.1 15.5 %collective-permute-start.1 = (bf16[256,1024]{1,0:T(8,128)(2,1)}, bf16[256,1024]{1,0:T(8,128)(2,1)}, u32[]{:S(2)}, u32[]{:S(2)}) collective-permute-start(bf16[256,1024]{1,0:T(8,128)(2,1)} %get-tuple-element.165), channel_id=1, source_target_pairs={{0,16},{16,0},{1,17},{17,1},{2,18},{18,2},{3,19},{19,3},{4,20},{20... | collective-permute-start | bytes 1572872 | tf_op jit(solution)/shard_map/ppermute | solution.py:964
  876.0 34.1 %collective-permute-start.9 = (bf16[4,128,1024]{2,1,0:T(8,128)(2,1)}, bf16[4,128,1024]{2,1,0:T(8,128)(2,1)}, u32[]{:S(2)}, u32[]{:S(2)}) collective-permute-start(bf16[4,128,1024]{2,1,0:T(8,128)(2,1)} %dynamic-slice_bitcast_fusion.1), channel_id=1, source_target_pairs={{0,16},{16,0},{1,17},{17,1},{2,18},{18,2},{3,19},{19,3},{4,20},{20... | collective-permute-start | bytes 3145736 | tf_op jit(solution)/shard_map/ppermute | solution.py:964
  879.0 30.4 %copy-start.10 = (bf16[1,64,640]{2,1,0:T(8,128)(2,1)S(1)}, bf16[1,64,640]{2,1,0:T(8,128)(2,1)}, u32[]{:S(2)}) copy-start(bf16[1,64,640]{2,1,0:T(8,128)(2,1)} %reduce-scatter.15.cloned.1.call-done) | copy-start | bytes 245764
  879.0 30.4 %copy-start.11 = (bf16[1,64,640]{2,1,0:T(8,128)(2,1)S(1)}, bf16[1,64,640]{2,1,0:T(8,128)(2,1)}, u32[]{:S(2)}) copy-start(bf16[1,64,640]{2,1,0:T(8,128)(2,1)} %reduce-scatter.17.cloned.1.call-done) | copy-start | bytes 245764
  880.0 29.4 %collective-permute-start.5 = (bf16[64,640]{1,0:T(8,128)(2,1)S(1)}, bf16[64,640]{1,0:T(8,128)(2,1)S(1)}, u32[]{:S(2)}, u32[]{:S(2)}) collective-permute-start(bf16[64,640]{1,0:T(8,128)(2,1)S(1)} %select_bitcast_fusion.6), channel_id=1, source_target_pairs={{0,16},{16,0},{1,17},{17,1},{2,18},{18,2},{3,19},{19,3},{4,20},{20... | collective-permute-start | bytes 245768 | tf_op jit(solution)/shard_map/ppermute | solution.py:964
  913.8 5.0 collective-permute-start.8
  916.2 5.0 collective-permute-start.14
  924.0 6.1 collective-permute-start.4
  938.8 8.2 collective-permute-start.11
  (16 other events, 111.8 us)
Sparse Core Ops, SparseCore 0:
  10.7 73.8 all-gather.8
  87.3 72.4 all-gather.10
  162.5 96.5 all-gather.6
  643.1 16.4 reduce-scatter.14
  661.7 18.3 reduce-scatter.16
  682.2 19.6 reduce-scatter.20
  704.2 19.8 reduce-scatter.18
  726.4 19.8 reduce-scatter.28
  748.6 19.8 reduce-scatter.26
  770.6 24.3 reduce-scatter.12
  797.4 24.0 reduce-scatter.10
  826.9 25.3 reduce-scatter.24
  912.8 24.8 reduce-scatter.22
